TPU v7x, 768 devices: a whole 4x8x12 slice. The times are simulated.
768 devices in a mesh: anc: 24 (over z, core), cand: 32 (over y, x).
Axes of the slice: x: 4, y: 8, z: 12, core: 2. Of those that a mesh axis runs over, the one named last changes fastest.
Arguments:
- anchors: bfloat16 [12288, 1536], P('anc'), may hold values from -0.5 to 0.5
- candidates: bfloat16 [30720, 1536], P('cand'), may hold values from -0.5 to 0.5
- anchor_group: int32 [12288], P('anc'), may hold values from 0 to 15359
- cand_group: int32 [30720], P('cand'), may hold values from 0 to 15359
- anchor_loss_cotangent: float32 [12288], P('anc'), may hold values from -6 to 6
Outputs:
- probe_costs: float32 [12288], P('anc')
- probe_derivatives: float32 [12288, 1536], P(('anc', 'cand'))
- grad_candidates: float32 [30720, 1536], P('cand', 'anc')
All inputs are finite; a program needn't handle non-finite values.
Results may differ from a plain program's by a relative error of at most 0.0048.
Values sent between devices are 32-bit elements; how exact they have to be, the bound alone decides.
No kernel may reach another device: no remote copies, remote signals or barrier semaphores. Data moves between devices by JAX's collectives and lax.ppermute only.
A program may use at most 64 MiB of HBM per device.

v0:
```python
import jax
import jax.numpy as jnp
from jax import lax
from jax.sharding import PartitionSpec as P

sharpness_scale = 0.05
epsilon = 1e-06


def normalize(rows):
    values = rows.astype(jnp.float32)
    radius = jnp.sqrt(jnp.sum(values * values, axis=1, keepdims=True) + epsilon)
    return (values / radius, radius)


def rescale_onto_sphere(term, unit, radius):
    inner = jnp.sum(unit * term, axis=1, keepdims=True)
    return (term - unit * inner) / radius


def per_device(anchors, candidates, anchor_group, cand_group, anchor_loss_cotangent):
    probe_direction, probe_length = normalize(anchors)
    pool_member_direction, pool_member_length = normalize(candidates)
    anchor_halfprec = probe_direction.astype(jnp.bfloat16)
    target_reduced_precision = pool_member_direction.astype(jnp.bfloat16)
    pairwise_logits = (
        jnp.dot(anchor_halfprec, target_reduced_precision.T, preferred_element_type=jnp.float32)
        / sharpness_scale
    )
    logit_exponentials = jnp.exp(pairwise_logits - 1.0 / sharpness_scale)
    matching_indicator = (anchor_group[:, None] == cand_group[None, :]).astype(jnp.float32)
    denominator_aggregate, paired_affinity_aggregate, paired_number = lax.psum(
        (
            jnp.sum(logit_exponentials, axis=1),
            jnp.sum(matching_indicator * pairwise_logits, axis=1),
            jnp.sum(matching_indicator, axis=1),
        ),
        "cand",
    )
    paired_number = jnp.maximum(paired_number, 1.0)
    probe_costs = (
        1.0 / sharpness_scale
        + jnp.log(denominator_aggregate)
        - paired_affinity_aggregate / paired_number
    )
    normalized_weight_factor = (
        anchor_loss_cotangent[:, None]
        * (
            logit_exponentials / denominator_aggregate[:, None]
            - matching_indicator / paired_number[:, None]
        )
        / sharpness_scale
    ).astype(jnp.bfloat16)
    anc_share = anchors.shape[0] // lax.axis_size("cand")
    anc_part = lax.psum_scatter(
        jnp.dot(
            normalized_weight_factor, target_reduced_precision, preferred_element_type=jnp.float32
        ),
        "cand",
        scatter_dimension=0,
        tiled=True,
    )
    anc_first = lax.axis_index("cand") * anc_share
    probe_derivatives = rescale_onto_sphere(
        anc_part,
        lax.dynamic_slice_in_dim(probe_direction, anc_first, anc_share, 0),
        lax.dynamic_slice_in_dim(probe_length, anc_first, anc_share, 0),
    )
    pool_member_contribution = lax.dot_general(
        normalized_weight_factor,
        anchor_halfprec,
        (((0,), (0,)), ((), ())),
        preferred_element_type=jnp.float32,
    )
    pool_member_slice = lax.psum_scatter(
        pool_member_contribution, "anc", scatter_dimension=1, tiled=True
    )
    col_width = pool_member_slice.shape[1]
    col_units = lax.dynamic_slice_in_dim(
        pool_member_direction, lax.axis_index("anc") * col_width, col_width, 1
    )
    inner = lax.psum(jnp.sum(col_units * pool_member_slice, axis=1), "anc")
    pool_member_slice = (pool_member_slice - col_units * inner[:, None]) / pool_member_length
    return (probe_costs, probe_derivatives, pool_member_slice)


def solution(mesh):
    in_specs = (P("anc", None), P("cand", None), P("anc"), P("cand"), P("anc"))
    out_specs = (P("anc"), P(("anc", "cand"), None), P("cand", "anc"))
    return jax.shard_map(
        per_device, mesh=mesh, in_specs=in_specs, out_specs=out_specs, check_vma=False
    )
```

profile of v0, /device:TPU:1, one launch (start us, length us, event | category | flops | bytes accessed | tf_op | source)
XLA Modules:
  0.0 472.8 jit_solution(16861558878446125134)
XLA Ops:
  7.2 0.0 reduce-scatter.3.cloned.1.call-start
  7.2 3.1 copy.8
  10.4 0.0 copy-start
  10.4 0.7 fusion
  11.1 0.6 copy-done
  11.8 0.4 fusion.1
  12.2 3.5 fusion.7
  15.7 62.9 %all-reduce = (f32[512]{0:T(512)S(1)}, f32[512]{0:T(512)S(1)}, f32[512]{0:T(512)S(1)}) all-reduce(f32[512]{0:T(512)S(1)} %get-tuple-element.4, f32[512]{0:T(512)S(1)} %get-tuple-element.3, f32[512]{0:T(512)S(1)} %get-tuple-element.5), channel_id=1, replica_groups=mesh['anc'=24,'cand'=32] {'cand'}, use_global_device_ids=true, to_apply=%region_5.0 | all-reduce | flops 1536 | bytes 12288 | tf_op jit(solution)/shard_map/psum | solution.py:32
  78.6 0.6 broadcast_maximum_fusion
  79.2 5.6 %fusion.8 = f32[512,1536]{1,0:T(8,128)} fusion(f32[512,960]{0,1:T(8,128)} %get-tuple-element.11, f32[512]{0:T(512)S(1)} %get-tuple-element.9, f32[512]{0:T(512)S(1)} %get-tuple-element.7, f32[512]{0:T(512)S(1)} %copy-done.3, s32[512]{0:T(512)S(1)} %copy-done.2, s32[960]{0:T(1024)S(1)} %copy-done.1, bf16[960,1536]{0,1:T(8,128)(2,1)S(1)} %copy.8, ...), kind=kOutput, calls=%fused_computation.16 | convolution fusion | flops 1519288320 | bytes 8076800 | tf_op jit(solution)/shard_map/dot_general | solution.py:56
  84.8 0.0 reduce-scatter.3.cloned.1.call-update
  84.9 0.0 reduce-scatter.5.cloned.1.call-start
  84.9 6.9 %fusion.12 = f32[960,1536]{0,1:T(8,128)} fusion(f32[512,960]{0,1:T(8,128)} %get-tuple-element.11, f32[512]{0:T(512)S(1)} %get-tuple-element.9, f32[512]{0:T(512)S(1)} %get-tuple-element.7, f32[512]{0:T(512)S(1)} %copy-done.3, s32[512]{0:T(512)S(1)} %copy-done.2, s32[960]{0:T(1024)S(1)} %copy-done.1, bf16[512,1536]{1,0:T(8,128)(2,1)} %param.5, ...), kind=kOutput, calls=%fused_computation.20 | convolution fusion | flops 1517223936 | bytes 9451264 | tf_op jit(solution)/shard_map/dot_general | solution.py:69
  91.8 0.0 reduce-scatter.5.cloned.1.call-update
  91.8 0.1 dynamic-slice.3
  91.9 3.5 convert_divide_fusion.1
  95.4 3.6 convert_divide_fusion
  99.0 226.5 %reduce-scatter.3.cloned.1.call-done = f32[16,1536]{1,0:T(8,128)} async-done(((f32[512,1536]{1,0:T(8,128)}), f32[16,1536]{1,0:T(8,128)}) %reduce-scatter.3.cloned.1.call-update) | async-done | bytes 98320 | tf_op jit(solution)/shard_map/reduce_scatter | solution.py:55
  325.4 1.1 multiply_reduce_fusion.1
  326.5 1.7 subtract_divide_fusion.1
  328.1 97.3 %reduce-scatter.5.cloned.1.call-done = f32[960,64]{0,1:T(8,128)} async-done(((f32[960,1536]{0,1:T(8,128)}), f32[960,64]{0,1:T(8,128)}) %reduce-scatter.5.cloned.1.call-update) | async-done | bytes 245776 | tf_op jit(solution)/shard_map/reduce_scatter | solution.py:75
  425.4 1.1 multiply_reduce_fusion
  426.5 37.8 %psum.31 = f32[960]{0:T(1024)S(1)} all-reduce(f32[960]{0:T(1024)S(1)} %multiply_reduce_fusion), channel_id=1, replica_groups=mesh['anc'=24,'cand'=32] {'anc'}, use_global_device_ids=true, to_apply=%region_12.0 | all-reduce | flops 960 | bytes 7680 | tf_op jit(solution)/shard_map/psum | solution.py:82
  464.2 1.8 subtract_divide_fusion
  (8 shorter events, 0.0 us)
Async XLA Ops:
  7.2 318.2 %reduce-scatter.3.cloned.1.call-start = ((), (), s32[]{:S(2)}) async-start(), calls=%async_computation.2 | async-start | bytes 3244032 | tf_op jit(solution)/shard_map/reduce_scatter | solution.py:55
  10.4 1.4 copy-start
  10.4 1.8 copy-start.1
  10.4 1.8 copy-start.2
  12.2 67.0 %copy-start.3 = (f32[512]{0:T(512)S(1)}, f32[512]{0:T(512)}, u32[]{:S(2)}) copy-start(f32[512]{0:T(512)} %param.9) | copy-start | bytes 6148
  84.9 340.6 %reduce-scatter.5.cloned.1.call-start = ((), (), s32[]{:S(2)}) async-start(), calls=%async_computation.3 | async-start | bytes 6553600 | tf_op jit(solution)/shard_map/reduce_scatter | solution.py:75
Sparse Core Ops, SparseCore 0:
  85.0 240.3 reduce-scatter.2
  328.9 96.5 reduce-scatter.4
where the time goes:
time: 473 us
  waiting for transfers between devices  324 us (68%)
  blocking collectives  101 us (21%)
  matrix products  16 us (3%)
  other arithmetic  14.4 us (3%)
  between operations  14.1 us (3%)
    reduce_scatter x1, waiting for transfers between devices, per_device(): lax.psum_scatter(jnp.dot(normalized_weight_factor, target_reduced_precisi...  226 us
    reduce_scatter x1, waiting for transfers between devices, per_device(): lax.psum_scatter(pool_member_contribution, 'anc', scatter_dimension=1, ti...  97.3 us
    psum x1, blocking collectives, per_device(): lax.psum((jnp.sum(logit_exponentials, axis=1), jnp.sum(matching_indicator...  62.9 us
    psum x1, blocking collectives, per_device(): inner = lax.psum(jnp.sum(col_units * pool_member_slice, axis=1), 'anc')  37.8 us
  transfers between devices with their start and end apart: 2, of which 2 were waited for; matrix products, arithmetic and copies ran while one was open for 4% of the time, Pallas kernels for 0%

commit v1 on v0

v1 whole, which is shorter than its diff:
```python
import functools

import jax
import jax.numpy as jnp
from jax import lax
from jax.experimental import pallas as pl
from jax.experimental.pallas import tpu as pltpu
from jax.sharding import PartitionSpec as P

SCALE = 20.0
EPS = 1e-06
F32 = jnp.float32
BF16 = jnp.bfloat16
NX, NY = 4, 8
LANES = 128
SLOTS = 16
VMEM = 62 * 2**20


def inverse_radius(values):
    return 1.0 / jnp.sqrt(jnp.sum(values * values, axis=1, keepdims=True) + EPS)


def score_kernel(a_ref, c_ref, ag_ref, cg_ref, an_ref, cn_ref, e_ref, st_ref, ir_ref, acc_ref):
    n = a_ref.shape[0]
    per = n // LANES

    @pl.when(pl.program_id(0) == 0)
    def _():
        for r in range(0, n, 128):
            values = a_ref[r : r + 128, :].astype(F32)
            an_ref[r : r + 128, :] = (values * inverse_radius(values)).astype(BF16)
        acc_ref[...] = jnp.zeros_like(acc_ref)

    values = c_ref[...].astype(F32)
    inv = inverse_radius(values)
    ir_ref[...] = jnp.broadcast_to(inv, ir_ref.shape)
    cn = (values * inv).astype(BF16)
    cn_ref[...] = cn
    scores = SCALE * lax.dot_general(
        cn, an_ref[...], (((1,), (1,)), ((), ())), preferred_element_type=F32
    )
    expo = jnp.exp(scores - SCALE)
    e_ref[...] = expo
    match = cg_ref[...] == ag_ref[...]
    sums = (
        jnp.sum(expo, axis=0, keepdims=True),
        jnp.sum(jnp.where(match, 1.0, 0.0), axis=0, keepdims=True),
        jnp.sum(jnp.where(match, scores, 0.0), axis=0, keepdims=True),
    )
    for k, s in enumerate(sums):
        for j in range(per):
            acc_ref[k * per + j : k * per + j + 1, :] += s[:, j * LANES : (j + 1) * LANES]

    @pl.when(pl.program_id(0) == pl.num_programs(0) - 1)
    def _():
        st_ref[...] = jnp.broadcast_to(acc_ref[...][None], st_ref.shape)


def score_stage(anchors, candidates, ag, cg, copies):
    n, width = anchors.shape
    m = candidates.shape[0]
    steps = 4
    rows = m // steps
    whole = lambda i: (0, 0)
    part = lambda i: (i, 0)
    return pl.pallas_call(
        score_kernel,
        grid=(steps,),
        in_specs=[
            pl.BlockSpec((n, width), whole),
            pl.BlockSpec((rows, width), part),
            pl.BlockSpec((1, n), whole),
            pl.BlockSpec((rows, 1), part),
        ],
        out_specs=[
            pl.BlockSpec((n, width), whole),
            pl.BlockSpec((rows, width), part),
            pl.BlockSpec((rows, n), part),
            pl.BlockSpec((copies, SLOTS, LANES), lambda i: (0, 0, 0)),
            pl.BlockSpec((rows, LANES), part),
        ],
        out_shape=[
            jax.ShapeDtypeStruct((n, width), BF16),
            jax.ShapeDtypeStruct((m, width), BF16),
            jax.ShapeDtypeStruct((m, n), F32),
            jax.ShapeDtypeStruct((copies, SLOTS, LANES), F32),
            jax.ShapeDtypeStruct((m, LANES), F32),
        ],
        scratch_shapes=[pltpu.VMEM((SLOTS, LANES), F32)],
        compiler_params=pltpu.CompilerParams(vmem_limit_bytes=VMEM),
        name="scores",
    )(anchors, candidates, ag, cg)


def candidate_kernel(
    core_ref, st_ref, cot_ref, ag_ref, cg_ref, e_ref, an_ref, c_ref, ir_ref,
    cost_ref, coef_ref, own_ref, oth_ref,
):
    n = ag_ref.shape[1]
    half = e_ref.shape[1]
    per = n // LANES
    st = jnp.sum(st_ref[...], axis=0)
    total, count, positive = (
        jnp.concatenate([st[k * per + j : k * per + j + 1, :] for j in range(per)], axis=1)
        for k in range(3)
    )
    count = jnp.maximum(count, 1.0)
    cost_ref[...] = SCALE + jnp.log(total) - positive / count
    cot = cot_ref[...] * SCALE
    per_total, per_count = 1.0 / total, 1.0 / count
    expo = e_ref[...].reshape(2 * half, n)
    match = cg_ref[...].reshape(2 * half, 1) == ag_ref[...]
    coef = (cot * (expo * per_total - jnp.where(match, per_count, 0.0))).astype(BF16)
    coef_ref[...] = coef.reshape(2, half, n)
    dcn = jnp.dot(coef, an_ref[...], preferred_element_type=F32)
    values = c_ref[...].reshape(2 * half, c_ref.shape[2]).astype(F32)
    inv = ir_ref[...].reshape(2 * half, LANES)[:, :1]
    inner = jnp.sum(values * dcn, axis=1, keepdims=True)
    grad = inv * (dcn - values * (inv * inv * inner))
    low = lax.broadcasted_iota(jnp.int32, (half, LANES), 1) < LANES // 2
    first = core_ref[0] == 0
    for z in range(own_ref.shape[0]):
        top = grad[:half, z * LANES : (z + 1) * LANES]
        bottom = grad[half:, z * LANES : (z + 1) * LANES]
        even = jnp.where(low, top, pltpu.roll(bottom, LANES // 2, 1))
        odd = jnp.where(low, pltpu.roll(top, LANES // 2, 1), bottom)
        own_ref[z] = jnp.where(first, even, odd)
        oth_ref[z] = jnp.where(first, odd, even)


def candidate_stage(core, st, cot, ag, cg, expo, an, candidates, ir):
    copies = st.shape[0]
    n, width = an.shape
    m = candidates.shape[0]
    blocks = width // LANES
    half = m // 2
    steps = 3
    rows = half // steps
    whole = lambda i: (0, 0)
    part = lambda i: (0, i, 0)
    packed = jax.ShapeDtypeStruct((blocks, half, LANES), F32)
    return pl.pallas_call(
        candidate_kernel,
        grid=(steps,),
        in_specs=[
            pl.BlockSpec(memory_space=pltpu.SMEM),
            pl.BlockSpec((copies, SLOTS, LANES), lambda i: (0, 0, 0)),
            pl.BlockSpec((1, n), whole),
            pl.BlockSpec((1, n), whole),
            pl.BlockSpec((2, rows, 1), part),
            pl.BlockSpec((2, rows, n), part),
            pl.BlockSpec((n, width), whole),
            pl.BlockSpec((2, rows, width), part),
            pl.BlockSpec((2, rows, LANES), part),
        ],
        out_specs=[
            pl.BlockSpec((1, n), whole),
            pl.BlockSpec((2, rows, n), part),
            pl.BlockSpec((blocks, rows, LANES), part),
            pl.BlockSpec((blocks, rows, LANES), part),
        ],
        out_shape=[
            jax.ShapeDtypeStruct((1, n), F32),
            jax.ShapeDtypeStruct((2, half, n), BF16),
            packed,
            packed,
        ],
        compiler_params=pltpu.CompilerParams(vmem_limit_bytes=VMEM),
        name="candidate_terms",
    )(
        core, st, cot, ag, cg.reshape(2, half, 1), expo.reshape(2, half, n), an,
        candidates.reshape(2, half, width), ir.reshape(2, half, LANES),
    )


def anchor_kernel(at_ref, coef_ref, cn_ref, xkeep, xsend, ykeep, ysend, scr):
    scr[...] = lax.dot_general(
        coef_ref[...], cn_ref[...], (((0,), (0,)), ((), ())), preferred_element_type=F32
    )
    share, cols = xkeep.shape[3:]
    x0, y0 = at_ref[0], at_ref[1]

    def rows(p, y, q, x):
        place = (2 * p + y) * NX + 2 * q + x
        return pl.ds(pl.multiple_of(place * share, share), share)

    for other in range(2):
        x, y = (x0, y0) if other == 0 else (1 - x0, 1 - y0)
        for p in range(NY // 2):
            for q in range(NX // 2):
                xkeep[other, p, q] = scr[rows(p, y, q, x0), :cols]
                xsend[other, p, q] = scr[rows(p, y, q, 1 - x0), :cols]
                ykeep[other, p, q] = scr[rows(p, y0, q, x), cols:]
                ysend[other, p, q] = scr[rows(p, 1 - y0, q, x), cols:]


def anchor_stage(at, coef, cn, share):
    width = cn.shape[1]
    n = coef.shape[1]
    part = jax.ShapeDtypeStruct((2, NY // 2, NX // 2, share, width // 2), F32)
    vmem = pl.BlockSpec(memory_space=pltpu.VMEM)
    return pl.pallas_call(
        anchor_kernel,
        in_specs=[pl.BlockSpec(memory_space=pltpu.SMEM), vmem, vmem],
        out_specs=[vmem] * 4,
        out_shape=[part] * 4,
        scratch_shapes=[pltpu.VMEM((n, width), F32)],
        compiler_params=pltpu.CompilerParams(vmem_limit_bytes=VMEM),
        name="anchor_terms",
    )(at, coef, cn)


def probe_kernel(t_ref, a_ref, o_ref):
    term = jnp.sum(t_ref[...], axis=0)
    values = a_ref[...].astype(F32)
    inv = inverse_radius(values)
    unit = values * inv
    o_ref[...] = (term - unit * jnp.sum(unit * term, axis=1, keepdims=True)) * inv


def probe_stage(terms, rows):
    return pl.pallas_call(
        probe_kernel,
        out_shape=jax.ShapeDtypeStruct(rows.shape, F32),
        name="probe_derivatives",
    )(terms, rows)


def unpack_kernel(p_ref, o_ref):
    half = p_ref.shape[0]
    t = p_ref[...].T
    o_ref[:, :half] = t[: LANES // 2]
    o_ref[:, half:] = t[LANES // 2 :]


def unpack_stage(packed):
    half = packed.shape[0]
    return pl.pallas_call(
        unpack_kernel,
        out_shape=jax.ShapeDtypeStruct((LANES // 2, 2 * half), F32),
        name="unpack",
    )(packed)


def per_device(n_anc, anchors, candidates, anchor_group, cand_group, cotangent):
    n, width = anchors.shape
    n_cand = NX * NY
    share = n // n_cand
    anc, cand = lax.axis_index("anc"), lax.axis_index("cand")
    core = anc % 2
    y, x = cand // NX, cand % NX

    def swap(v, over_x):
        pairs = []
        for p in range(n_anc):
            for j in range(NY):
                for i in range(NX):
                    k = i if over_x else j
                    k += 1 if (k - p) % 2 == 0 else -1
                    to = j * NX + k % NX if over_x else (k % NY) * NX + i
                    pairs.append((p * n_cand + j * NX + i, p * n_cand + to))
        return lax.ppermute(v, ("anc", "cand"), pairs)

    ag, cg = anchor_group.reshape(1, n), cand_group.reshape(-1, 1)
    an, cn, expo, st, ir = score_stage(anchors, candidates, ag, cg, n_cand)
    st = lax.all_to_all(st, "cand", 0, 0, tiled=True)
    cost, coef, own, oth = candidate_stage(
        core.reshape(1).astype(jnp.int32), st, cotangent.reshape(1, n), ag, cg, expo, an,
        candidates, ir,
    )

    sibling = lax.ppermute(oth, "anc", [(p, p ^ 1) for p in range(n_anc)])
    packed = lax.psum_scatter(
        own + sibling, "anc", scatter_dimension=0,
        axis_index_groups=[list(range(c, n_anc, 2)) for c in range(2)], tiled=False,
    )
    grad_candidates = unpack_stage(packed).T

    at = jnp.stack([x % 2, y % 2]).astype(jnp.int32)
    xkeep, xsend, ykeep, ysend = anchor_stage(at, coef.reshape(-1, n), cn, share)
    xgot, ygot = swap(xsend, True), swap(ysend, False)
    xagain, yagain = swap(xkeep[1] + xgot[1], False), swap(ykeep[1] + ygot[1], True)
    xpart, ypart = xkeep[0] + xgot[0] + xagain, ykeep[0] + ygot[0] + yagain
    groups = [
        [(2 * p + j) * NX + 2 * q + i for p in range(NY // 2) for q in range(NX // 2)]
        for j in range(2) for i in range(2)
    ]
    terms = jnp.concatenate([xpart, ypart], axis=-1).reshape(-1, share, width)
    terms = lax.all_to_all(terms, "cand", 0, 0, axis_index_groups=groups, tiled=True)
    rows = lax.dynamic_slice_in_dim(anchors, cand * share, share, 0)
    probe_derivatives = probe_stage(terms, rows)
    return cost.reshape(n), probe_derivatives, grad_candidates


def solution(mesh):
    in_specs = (P("anc", None), P("cand", None), P("anc"), P("cand"), P("anc"))
    out_specs = (P("anc"), P(("anc", "cand"), None), P("cand", "anc"))
    return jax.shard_map(
        functools.partial(per_device, mesh.shape["anc"]),
        mesh=mesh, in_specs=in_specs, out_specs=out_specs, check_vma=False,
    )
```

time: 473 us -> 139 us (0.29)
  waiting for transfers between devices: 324 us -> 49 us
  blocking collectives: 101 us -> 0 us
  starting transfers between devices: 0.08 us -> 32.5 us
  Pallas kernels: 0 us -> 26.6 us
  matrix products: 16 us -> 0 us
  other arithmetic: 14.4 us -> 8.64 us
    reduce_scatter x2 -> x1, waiting for transfers between devices: 324 us -> 0.01 us  [per_device(): lax.psum_scatter(own + sibling, 'anc', scatter_dimension=0, axis_index_gr...]
    psum x2 -> x0, blocking collectives: 101 us -> none  [the longest x1 62.9 us: per_device(): lax.psum((jnp.sum(logit_exponentials, axis=1), jnp.sum(matching_indicator...]
    all_to_all x0 -> x2, waiting for transfers between devices: none -> 29.1 us  [the longest x1 19.8 us: per_device(): lax.all_to_all(terms, 'cand', 0, 0, axis_index_groups=groups, tiled=True)]
    pallas_call x0 -> x5, Pallas kernels: none -> 26.6 us  [the longest x1 8.88 us: candidate_stage(): pl.pallas_call(candidate_kernel, grid=(steps,), in_specs=[pl.BlockSpec(me...]
    ppermute x0 -> x5, waiting for transfers between devices: none -> 19.8 us  [the longest x4 14.6 us: swap(): return lax.ppermute(v, ('anc', 'cand'), pairs)]
    ppermute x0 -> x5, starting transfers between devices: none -> 17.7 us  [the longest x4 10.7 us: swap(): return lax.ppermute(v, ('anc', 'cand'), pairs)]
    dot_general x3 -> x0, matrix products: 16 us -> none  [the longest x1 6.86 us: per_device(): lax.dot_general(normalized_weight_factor, anchor_halfprec, (((0,), (0,)),...]
    all_to_all x0 -> x2, starting transfers between devices: none -> 14.8 us  [the longest x1 10.5 us: per_device(): st = lax.all_to_all(st, 'cand', 0, 0, tiled=True)]
  transfers between devices with their start and end apart: 2 -> 8, of which waited for: 2 -> 6; matrix products, arithmetic and copies ran while one was open for 4% -> 5% of each run, Pallas kernels for 0% -> 6%
where the time goes in v1:
time: 139 us; the launch traced here: 137 us
  waiting for transfers between devices  49 us (35%)
  starting transfers between devices  32.5 us (23%)
  Pallas kernels  26.6 us (19%)
  between operations  14.2 us (10%)
  other arithmetic  8.64 us (6%)
  local copies, waits for them, and re-layouts  5.91 us (4%)
    all_to_all x1, waiting for transfers between devices, per_device(): lax.all_to_all(terms, 'cand', 0, 0, axis_index_groups=groups, tiled=True)  19.8 us
    ppermute x4, waiting for transfers between devices, swap(): return lax.ppermute(v, ('anc', 'cand'), pairs)  14.6 us
    ppermute x4, starting transfers between devices, swap(): return lax.ppermute(v, ('anc', 'cand'), pairs)  10.7 us
    all_to_all x1, starting transfers between devices, per_device(): st = lax.all_to_all(st, 'cand', 0, 0, tiled=True)  10.5 us
    all_to_all x1, waiting for transfers between devices, per_device(): st = lax.all_to_all(st, 'cand', 0, 0, tiled=True)  9.32 us
    pallas_call x1, Pallas kernels, candidate_stage(): pl.pallas_call(candidate_kernel, grid=(steps,), in_specs=[pl.BlockSpec(me...  8.88 us
    pallas_call x1, Pallas kernels, score_stage(): pl.pallas_call(score_kernel, grid=(steps,), in_specs=[pl.BlockSpec((n, wi...  8.14 us
    ppermute x1, starting transfers between devices, per_device(): sibling = lax.ppermute(oth, 'anc', [(p, p ^ 1) for p in range(n_anc)])  7.01 us
  transfers between devices with their start and end apart: 8, of which 6 were waited for; matrix products, arithmetic and copies ran while one was open for 5% of the time, Pallas kernels for 6%

profile of v1, /device:TPU:1, one launch (start us, length us, event | category | flops | bytes accessed | tf_op | source)
XLA Modules:
  0.0 136.8 jit_solution(13896325508848270273)
XLA Ops:
  7.2 1.8 %copy.8.cg_ref = s32[960,1]{1,0:T(8,128)} copy(s32[960,1]{0,1:T(1,128)} %bitcast.32) | data formatting | bytes 7680 | tf_op jit(solution)/shard_map/reshape | solution.py:265
  8.9 8.1 %scores.1 = (bf16[512,1536]{1,0:T(8,128)(2,1)}, bf16[960,1536]{1,0:T(8,128)(2,1)}, f32[960,512]{1,0:T(8,128)}, f32[32,16,128]{2,1,0:T(8,128)}, f32[960,128]{1,0:T(8,128)}) custom-call(bf16[512,1536]{1,0:T(8,128)(2,1)} %a_ref.1, bf16[960,1536]{1,0:T(8,128)(2,1)} %c_ref.1, s32[1,512]{1,0:T(1,128)} %bitcast.33, s32[960,1]{1,0:T(8,128)} %copy.8.cg_ref), custom_call_target="tpu_custom_call" | custom-call | tf_op jit(solution)/shard_map/scores/pallas_call | solution.py:67
  17.1 10.5 %all-to-all-start = ((f32[32,16,128]{2,1,0:T(8,128)}), f32[32,16,128]{2,1,0:T(8,128)S(1)}, u32[]{:S(2)}, u32[]{:S(2)}) async-start(f32[32,16,128]{2,1,0:T(8,128)} %get-tuple-element.16), calls=%async_computation | async-start | bytes 524288 | tf_op jit(solution)/shard_map/all_to_all | solution.py:267
  27.7 1.1 reshape_reshape.4.cg_ref
  28.8 9.3 %all-to-all-done.st_ref = f32[32,16,128]{2,1,0:T(8,128)S(1)} async-done(((f32[32,16,128]{2,1,0:T(8,128)}), f32[32,16,128]{2,1,0:T(8,128)S(1)}, u32[]{:S(2)}, u32[]{:S(2)}) %all-to-all-start) | async-done | bytes 262176 | tf_op jit(solution)/shard_map/all_to_all | solution.py:267
  38.8 8.9 %candidate_terms.1 = (f32[1,512]{1,0:T(1,128)}, bf16[2,480,512]{2,1,0:T(8,128)(2,1)}, f32[12,480,128]{2,1,0:T(8,128)}, f32[12,480,128]{2,1,0:T(8,128)}) custom-call(s32[1]{0:T(128)} %bitcast.core_ref, f32[32,16,128]{2,1,0:T(8,128)} %copy-done.1, f32[1,512]{1,0:T(1,128)} %bitcast.35, s32[1,512]{1,0:T(1,128)} %bitcast.34, s32[2,480,1]{2,1,0:T(8,128)} %reshape_reshape.4.cg_ref, ...), custom_call_target="tpu_custom_call" | custom-call | tf_op jit(solution)/shard_map/candidate_terms/pallas_call | solution.py:143
  47.7 7.0 %collective-permute-start.4 = (f32[12,480,128]{2,1,0:T(8,128)}, f32[12,480,128]{2,1,0:T(8,128)S(1)}, u32[]{:S(2)}, u32[]{:S(2)}) collective-permute-start(f32[12,480,128]{2,1,0:T(8,128)} %get-tuple-element.28), channel_id=1, source_target_pairs={{0,32},{32,0},{64,96},{96,64},{128,160},{160,128},{192,224},{224,1... | collective-permute-start | bytes 8847368 | tf_op jit(solution)/shard_map/ppermute | solution.py:273
  54.7 5.2 %collective-permute-done.4 = f32[12,480,128]{2,1,0:T(8,128)S(1)} collective-permute-done((f32[12,480,128]{2,1,0:T(8,128)}, f32[12,480,128]{2,1,0:T(8,128)S(1)}, u32[]{:S(2)}, u32[]{:S(2)}) %collective-permute-start.4) | collective-permute-done | bytes 2949152 | tf_op jit(solution)/shard_map/ppermute | solution.py:273
  59.9 3.7 %add.67 = f32[12,480,128]{2,1,0:T(8,128)} add(f32[12,480,128]{2,1,0:T(8,128)} %get-tuple-element.27, f32[12,480,128]{2,1,0:T(8,128)S(1)} %collective-permute-done.4) | non-fusion elementwise | flops 737280 | bytes 8847360 | tf_op jit(solution)/shard_map/add | solution.py:275
  64.4 5.7 %anchor_terms.1 = (f32[2,4,2,16,768]{4,3,2,1,0:T(8,128)}, f32[2,4,2,16,768]{4,3,2,1,0:T(8,128)}, f32[2,4,2,16,768]{4,3,2,1,0:T(8,128)}, f32[2,4,2,16,768]{4,3,2,1,0:T(8,128)}) custom-call(s32[2]{0:T(128)} %pad_add_fusion.at_ref, bf16[960,512]{1,0:T(8,128)(2,1)} %bitcast.28, bf16[960,1536]{1,0:T(8,128)(2,1)} %get-tuple-element.22.cn_ref), custom_call_target="tpu_custom_call" | custom-call | tf_op jit(solution)/shard_map/anchor_terms/pallas_call | solution.py:203
  70.1 2.9 %collective-permute-start = (f32[2,4,2,16,768]{4,3,2,1,0:T(8,128)}, f32[2,4,2,16,768]{4,3,2,1,0:T(8,128)S(1)}, u32[]{:S(2)}, u32[]{:S(2)}) collective-permute-start(f32[2,4,2,16,768]{4,3,2,1,0:T(8,128)} %get-tuple-element.24), channel_id=1, source_target_pairs={{0,1},{1,0},{2,3},{3,2},{4,5},{5,4},{6,7},{7,6},{8,9},{9,8},{10,11... | collective-permute-start | bytes 2359304 | tf_op jit(solution)/shard_map/ppermute | solution.py:263
  73.0 1.9 %collective-permute-start.2 = (f32[2,4,2,16,768]{4,3,2,1,0:T(8,128)}, f32[2,4,2,16,768]{4,3,2,1,0:T(8,128)S(1)}, u32[]{:S(2)}, u32[]{:S(2)}) collective-permute-start(f32[2,4,2,16,768]{4,3,2,1,0:T(8,128)} %get-tuple-element.26), channel_id=1, source_target_pairs={{0,4},{1,5},{2,6},{3,7},{4,0},{5,1},{6,2},{7,3},{8,12},{9,13},{10,... | collective-permute-start | bytes 2359304 | tf_op jit(solution)/shard_map/ppermute | solution.py:263
  74.9 9.4 %collective-permute-done = f32[2,4,2,16,768]{4,3,2,1,0:T(8,128)S(1)} collective-permute-done((f32[2,4,2,16,768]{4,3,2,1,0:T(8,128)}, f32[2,4,2,16,768]{4,3,2,1,0:T(8,128)S(1)}, u32[]{:S(2)}, u32[]{:S(2)}) %collective-permute-start) | collective-permute-done | bytes 786464 | tf_op jit(solution)/shard_map/ppermute | solution.py:263
  85.4 2.0 %collective-permute-start.1 = (f32[4,2,16,768]{3,2,1,0:T(8,128)S(1)}, f32[4,2,16,768]{3,2,1,0:T(8,128)S(1)}, u32[]{:S(2)}, u32[]{:S(2)}) collective-permute-start(f32[4,2,16,768]{3,2,1,0:T(8,128)S(1)} %fusion.3), channel_id=1, source_target_pairs={{0,4},{1,5},{2,6},{3,7},{4,0},{5,1},{6,2},{7,3},{8,12},{9,13},{10,... | collective-permute-start | bytes 1179656 | tf_op jit(solution)/shard_map/ppermute | solution.py:263
  87.4 1.1 fusion
  88.5 3.9 %collective-permute-start.3 = (f32[4,2,16,768]{3,2,1,0:T(8,128)S(1)}, f32[4,2,16,768]{3,2,1,0:T(8,128)S(1)}, u32[]{:S(2)}, u32[]{:S(2)}) collective-permute-start(f32[4,2,16,768]{3,2,1,0:T(8,128)S(1)} %fusion), channel_id=1, source_target_pairs={{0,1},{1,0},{2,3},{3,2},{4,5},{5,4},{6,7},{7,6},{8,9},{9,8},{10,11... | collective-permute-start | bytes 1179656 | tf_op jit(solution)/shard_map/ppermute | solution.py:263
  92.3 3.0 %collective-permute-done.1 = f32[4,2,16,768]{3,2,1,0:T(8,128)S(1)} collective-permute-done((f32[4,2,16,768]{3,2,1,0:T(8,128)S(1)}, f32[4,2,16,768]{3,2,1,0:T(8,128)S(1)}, u32[]{:S(2)}, u32[]{:S(2)}) %collective-permute-start.1) | collective-permute-done | bytes 393248 | tf_op jit(solution)/shard_map/ppermute | solution.py:263
  95.3 1.1 fusion.5
  96.4 2.2 %collective-permute-done.3 = f32[4,2,16,768]{3,2,1,0:T(8,128)S(1)} collective-permute-done((f32[4,2,16,768]{3,2,1,0:T(8,128)S(1)}, f32[4,2,16,768]{3,2,1,0:T(8,128)S(1)}, u32[]{:S(2)}, u32[]{:S(2)}) %collective-permute-start.3) | collective-permute-done | bytes 393248 | tf_op jit(solution)/shard_map/ppermute | solution.py:263
  99.6 4.3 %all-to-all-start.1 = ((f32[8,16,1536]{2,1,0:T(8,128)}), f32[8,16,1536]{2,1,0:T(8,128)S(1)}, u32[]{:S(2)}, u32[]{:S(2)}) async-start(f32[8,16,1536]{2,1,0:T(8,128)} %bitcast.15), calls=%async_computation.1 | async-start | bytes 1572864 | tf_op jit(solution)/shard_map/all_to_all | solution.py:290
  104.0 1.4 %constant_dynamic-slice_fusion.a_ref = bf16[16,1536]{1,0:T(8,128)(2,1)} fusion(bf16[512,1536]{1,0:T(8,128)(2,1)} %a_ref.1, s32[]{:T(128)S(6)} %select_n.31), kind=kLoop, calls=%fused_computation.12 | loop fusion | bytes 98308 | tf_op jit(solution)/shard_map/dynamic_slice | solution.py:291
  105.4 19.8 %all-to-all-done.1.t_ref = f32[8,16,1536]{2,1,0:T(8,128)S(1)} async-done(((f32[8,16,1536]{2,1,0:T(8,128)}), f32[8,16,1536]{2,1,0:T(8,128)S(1)}, u32[]{:S(2)}, u32[]{:S(2)}) %all-to-all-start.1) | async-done | bytes 786464 | tf_op jit(solution)/shard_map/all_to_all | solution.py:290
  126.1 2.0 %probe_derivatives.1 = f32[16,1536]{1,0:T(8,128)} custom-call(f32[8,16,1536]{2,1,0:T(8,128)} %copy-done, bf16[16,1536]{1,0:T(8,128)(2,1)} %constant_dynamic-slice_fusion.a_ref), custom_call_target="tpu_custom_call" | custom-call | tf_op jit(solution)/shard_map/probe_derivatives/pallas_call | solution.py:223
  128.1 1.9 %unpack.1 = f32[64,960]{1,0:T(8,128)} custom-call(f32[480,128]{1,0:T(8,128)} %bitcast.31), custom_call_target="tpu_custom_call" | custom-call | tf_op jit(solution)/shard_map/unpack/pallas_call | solution.py:239
  (16 shorter events, 4.4 us)
Async XLA Ops:
  7.2 20.5 %copy-start.3 = (s32[960]{0:T(1024)S(1)}, s32[960]{0:T(1024)}, u32[]{:S(2)}) copy-start(s32[960]{0:T(1024)} %param.8) | copy-start | bytes 11524
  17.1 21.0 %all-to-all-start = ((f32[32,16,128]{2,1,0:T(8,128)}), f32[32,16,128]{2,1,0:T(8,128)S(1)}, u32[]{:S(2)}, u32[]{:S(2)}) async-start(f32[32,16,128]{2,1,0:T(8,128)} %get-tuple-element.16), calls=%async_computation | async-start | bytes 524288 | tf_op jit(solution)/shard_map/all_to_all | solution.py:267
  27.6 100.5 %reduce-scatter.2.cloned.1.call-start = ((), (), s32[]{:S(2)}) async-start(), calls=%async_computation.3 | async-start | bytes 3194880 | tf_op jit(solution)/shard_map/reduce_scatter | solution.py:274
  38.1 0.7 copy-start.1
  47.7 12.2 %collective-permute-start.4 = (f32[12,480,128]{2,1,0:T(8,128)}, f32[12,480,128]{2,1,0:T(8,128)S(1)}, u32[]{:S(2)}, u32[]{:S(2)}) collective-permute-start(f32[12,480,128]{2,1,0:T(8,128)} %get-tuple-element.28), channel_id=1, source_target_pairs={{0,32},{32,0},{64,96},{96,64},{128,160},{160,128},{192,224},{224,1... | collective-permute-start | bytes 8847368 | tf_op jit(solution)/shard_map/ppermute | solution.py:273
  70.1 28.5 %copy-start.2 = (f32[2,4,2,16,768]{4,3,2,1,0:T(8,128)S(1)}, f32[2,4,2,16,768]{4,3,2,1,0:T(8,128)}, u32[]{:S(2)}) copy-start(f32[2,4,2,16,768]{4,3,2,1,0:T(8,128)} %get-tuple-element.25) | copy-start | bytes 2359300
  70.1 14.3 %collective-permute-start = (f32[2,4,2,16,768]{4,3,2,1,0:T(8,128)}, f32[2,4,2,16,768]{4,3,2,1,0:T(8,128)S(1)}, u32[]{:S(2)}, u32[]{:S(2)}) collective-permute-start(f32[2,4,2,16,768]{4,3,2,1,0:T(8,128)} %get-tuple-element.24), channel_id=1, source_target_pairs={{0,1},{1,0},{2,3},{3,2},{4,5},{5,4},{6,7},{7,6},{8,9},{9,8},{10,11... | collective-permute-start | bytes 2359304 | tf_op jit(solution)/shard_map/ppermute | solution.py:263
  73.0 14.4 %collective-permute-start.2 = (f32[2,4,2,16,768]{4,3,2,1,0:T(8,128)}, f32[2,4,2,16,768]{4,3,2,1,0:T(8,128)S(1)}, u32[]{:S(2)}, u32[]{:S(2)}) collective-permute-start(f32[2,4,2,16,768]{4,3,2,1,0:T(8,128)} %get-tuple-element.26), channel_id=1, source_target_pairs={{0,4},{1,5},{2,6},{3,7},{4,0},{5,1},{6,2},{7,3},{8,12},{9,13},{10,... | collective-permute-start | bytes 2359304 | tf_op jit(solution)/shard_map/ppermute | solution.py:263
  85.4 9.9 %collective-permute-start.1 = (f32[4,2,16,768]{3,2,1,0:T(8,128)S(1)}, f32[4,2,16,768]{3,2,1,0:T(8,128)S(1)}, u32[]{:S(2)}, u32[]{:S(2)}) collective-permute-start(f32[4,2,16,768]{3,2,1,0:T(8,128)S(1)} %fusion.3), channel_id=1, source_target_pairs={{0,4},{1,5},{2,6},{3,7},{4,0},{5,1},{6,2},{7,3},{8,12},{9,13},{10,... | collective-permute-start | bytes 1179656 | tf_op jit(solution)/shard_map/ppermute | solution.py:263
  88.5 10.1 %collective-permute-start.3 = (f32[4,2,16,768]{3,2,1,0:T(8,128)S(1)}, f32[4,2,16,768]{3,2,1,0:T(8,128)S(1)}, u32[]{:S(2)}, u32[]{:S(2)}) collective-permute-start(f32[4,2,16,768]{3,2,1,0:T(8,128)S(1)} %fusion), channel_id=1, source_target_pairs={{0,1},{1,0},{2,3},{3,2},{4,5},{5,4},{6,7},{7,6},{8,9},{9,8},{10,11... | collective-permute-start | bytes 1179656 | tf_op jit(solution)/shard_map/ppermute | solution.py:263
  99.6 25.6 %all-to-all-start.1 = ((f32[8,16,1536]{2,1,0:T(8,128)}), f32[8,16,1536]{2,1,0:T(8,128)S(1)}, u32[]{:S(2)}, u32[]{:S(2)}) async-start(f32[8,16,1536]{2,1,0:T(8,128)} %bitcast.15), calls=%async_computation.1 | async-start | bytes 1572864 | tf_op jit(solution)/shard_map/all_to_all | solution.py:290
  125.2 0.9 copy-start
Sparse Core Ops, SparseCore 0:
  63.8 55.7 reduce-scatter.1

commit v2 on v1

v2 whole, which is shorter than its diff:
```python
import functools

import jax
import jax.numpy as jnp
from jax import lax
from jax.experimental import pallas as pl
from jax.experimental.pallas import tpu as pltpu
from jax.sharding import PartitionSpec as P

SCALE = 20.0
EPS = 1e-06
F32 = jnp.float32
BF16 = jnp.bfloat16
NX, NY = 4, 8
LANES = 128
SLOTS = 12
MIB = 2**20
VMEM = pl.BlockSpec(memory_space=pltpu.VMEM)
HBM = pl.BlockSpec(memory_space=pltpu.HBM)
SMEM = pl.BlockSpec(memory_space=pltpu.SMEM)


def inverse_radius(values):
    return 1.0 / jnp.sqrt(jnp.sum(values * values, axis=1, keepdims=True) + EPS)


class Copies:
    def __init__(self, sems):
        self.sems, self.all = sems, []

    def start(self, source, target):
        copy = pltpu.make_async_copy(source, target, self.sems.at[len(self.all)])
        copy.start()
        self.all.append(copy)
        return copy


SCORE_STEPS = 4
SCORE_COPIES = 3 + 4 * SCORE_STEPS


def score_kernel(
    a_hbm, c_hbm, ag_ref, cg_ref, an_hbm, cn_hbm, e_hbm, st_hbm, row_hbm,
    a_ref, c_ref, an_ref, cn_ref, e_ref, st_ref, row_ref, acc_ref, sems,
):
    n, m = a_ref.shape[0], c_ref.shape[0]
    per = n // LANES
    rows = m // SCORE_STEPS
    parts = [pl.ds(k * rows, rows) for k in range(SCORE_STEPS)]
    copies = Copies(sems)
    a_copy = copies.start(a_hbm, a_ref)
    c_copies = [copies.start(c_hbm.at[part], c_ref.at[part]) for part in parts]
    out = []
    for k in range(0, m, LANES):
        size = min(LANES, m - k)
        row_ref[k : k + size, :] = jnp.broadcast_to(
            cg_ref[:, k : k + size].astype(F32), (LANES, size)
        ).T
    a_copy.wait()
    for r in range(0, n, LANES):
        values = a_ref[r : r + LANES, :].astype(F32)
        an_ref[r : r + LANES, :] = (values * inverse_radius(values)).astype(BF16)
    out.append(copies.start(an_ref, an_hbm))
    ag = ag_ref[...].astype(F32)
    left = lax.broadcasted_iota(jnp.int32, (rows, LANES), 1) < LANES // 2
    acc = None
    for part, c_copy in zip(parts, c_copies):
        c_copy.wait()
        values = c_ref[part, :].astype(F32)
        inv = inverse_radius(values)
        cn = (values * inv).astype(BF16)
        cn_ref[part, :] = cn
        out.append(copies.start(cn_ref.at[part], cn_hbm.at[part]))
        scores = SCALE * lax.dot_general(
            cn, an_ref[...], (((1,), (1,)), ((), ())), preferred_element_type=F32
        )
        expo = jnp.exp(scores - SCALE)
        e_ref[part, :] = expo
        out.append(copies.start(e_ref.at[part], e_hbm.at[part]))
        group = row_ref[part, :]
        row_ref[part, :] = jnp.where(left, inv, group)
        out.append(copies.start(row_ref.at[part], row_hbm.at[part]))
        match = group[:, LANES - 1 :] == ag
        sums = (
            jnp.sum(expo, axis=0, keepdims=True),
            jnp.sum(jnp.where(match, 1.0, 0.0), axis=0, keepdims=True),
            jnp.sum(jnp.where(match, scores, 0.0), axis=0, keepdims=True),
        )
        acc = sums if acc is None else tuple(u + v for u, v in zip(acc, sums))
    for k, s in enumerate(acc):
        for j in range(per):
            acc_ref[k * per + j : k * per + j + 1, :] = s[:, j * LANES : (j + 1) * LANES]
    st_ref[...] = jnp.broadcast_to(acc_ref[...][None], st_ref.shape)
    out.append(copies.start(st_ref, st_hbm))
    for copy in out:
        copy.wait()


def score_stage(anchors, candidates, ag, cg, copies):
    n, width = anchors.shape
    m = candidates.shape[0]
    shapes = [
        ((n, width), BF16),
        ((m, width), BF16),
        ((m, n), F32),
        ((copies, SLOTS, LANES), F32),
        ((m, LANES), F32),
    ]
    return pl.pallas_call(
        score_kernel,
        in_specs=[HBM, HBM, VMEM, VMEM],
        out_specs=[HBM] * 5,
        out_shape=[jax.ShapeDtypeStruct(*s) for s in shapes],
        scratch_shapes=[
            pltpu.VMEM((n, width), BF16),
            pltpu.VMEM((m, width), BF16),
            *(pltpu.VMEM(*s) for s in shapes),
            pltpu.VMEM((SLOTS, LANES), F32),
            pltpu.SemaphoreType.DMA((SCORE_COPIES,)),
        ],
        compiler_params=pltpu.CompilerParams(vmem_limit_bytes=62 * MIB),
        name="scores",
    )(anchors, candidates, ag, cg)


CANDIDATE_STEPS = 3
CANDIDATE_COPIES = 2 + 6 * CANDIDATE_STEPS


def candidate_kernel(
    at_ref, st_hbm, cot_ref, ag_ref, row_hbm, e_hbm, an_hbm, c_hbm,
    cost_ref, coef_hbm, own_hbm, oth_hbm,
    st_ref, row_ref, e_ref, an_ref, c_ref, coef_ref, own_ref, oth_ref, sems,
):
    n = ag_ref.shape[1]
    half = own_ref.shape[1]
    rows = half // CANDIDATE_STEPS
    per = n // LANES
    parts = [pl.ds(k * rows, rows) for k in range(CANDIDATE_STEPS)]
    copies = Copies(sems)
    st_copy = copies.start(st_hbm, st_ref)
    ready = []
    for k, part in enumerate(parts):
        ready.append([
            copies.start(ref.at[:, part], to.at[:, part])
            for ref, to in ((row_hbm, row_ref), (e_hbm, e_ref), (c_hbm, c_ref))
        ])
        if k == 0:
            an_copy = copies.start(an_hbm, an_ref)
    out = []
    st_copy.wait()
    st = jnp.sum(st_ref[...], axis=0)
    total, count, positive = (
        jnp.concatenate([st[k * per + j : k * per + j + 1, :] for j in range(per)], axis=1)
        for k in range(3)
    )
    count = jnp.maximum(count, 1.0)
    cost_ref[...] = SCALE + jnp.log(total) - positive / count
    cot = cot_ref[...] * SCALE
    per_total, per_count = 1.0 / total, 1.0 / count
    ag = ag_ref[...].astype(F32)
    low = lax.broadcasted_iota(jnp.int32, (rows, LANES), 1) < LANES // 2
    first = at_ref[2] == 0

    def coefficients(side, part):
        match = row_ref[side, part, LANES - 1 :] == ag
        coef = (cot * (e_ref[side, part, :] * per_total - jnp.where(match, per_count, 0.0))).astype(BF16)
        coef_ref[side, part, :] = coef
        return coef

    def terms(side, part, coef):
        dcn = jnp.dot(coef, an_ref[...], preferred_element_type=F32)
        values = c_ref[side, part, :].astype(F32)
        inv = row_ref[side, part, :1]
        inner = jnp.sum(values * dcn, axis=1, keepdims=True)
        return inv * (dcn - values * (inv * inv * inner))

    for k, part in enumerate(parts):
        for copy in ready[k]:
            copy.wait()
        coefs = [coefficients(side, part) for side in range(2)]
        out.append(copies.start(coef_ref.at[:, part], coef_hbm.at[:, part]))
        if k == 0:
            an_copy.wait()
        over, under = (terms(side, part, coefs[side]) for side in range(2))
        for z in range(own_ref.shape[0]):
            top = over[:, z * LANES : (z + 1) * LANES]
            bottom = under[:, z * LANES : (z + 1) * LANES]
            even = jnp.where(low, top, pltpu.roll(bottom, LANES // 2, 1))
            odd = jnp.where(low, pltpu.roll(top, LANES // 2, 1), bottom)
            own_ref[z, part, :] = jnp.where(first, even, odd)
            oth_ref[z, part, :] = jnp.where(first, odd, even)
        out.append(copies.start(oth_ref.at[:, part], oth_hbm.at[:, part]))
        out.append(copies.start(own_ref.at[:, part], own_hbm.at[:, part]))
    for copy in out:
        copy.wait()


def candidate_stage(at, st, cot, ag, row, expo, an, candidates):
    n, width = an.shape
    half = candidates.shape[0] // 2
    ins = [
        (st.shape, F32),
        ((2, half, LANES), F32),
        ((2, half, n), F32),
        ((n, width), BF16),
        ((2, half, width), BF16),
    ]
    outs = [((2, half, n), BF16)] + [((width // LANES, half, LANES), F32)] * 2
    return pl.pallas_call(
        candidate_kernel,
        in_specs=[SMEM, HBM, VMEM, VMEM, HBM, HBM, HBM, HBM],
        out_specs=[VMEM, HBM, HBM, HBM],
        out_shape=[jax.ShapeDtypeStruct((1, n), F32)] + [jax.ShapeDtypeStruct(*s) for s in outs],
        scratch_shapes=[
            *(pltpu.VMEM(*s) for s in ins + outs),
            pltpu.SemaphoreType.DMA((CANDIDATE_COPIES,)),
        ],
        compiler_params=pltpu.CompilerParams(vmem_limit_bytes=61 * MIB),
        name="candidate_terms",
    )(
        at, st, cot, ag, row.reshape(ins[1][0]), expo.reshape(ins[2][0]), an,
        candidates.reshape(ins[4][0]),
    )


def anchor_kernel(at_ref, coef_hbm, cn_hbm, xkeep, xsend, ykeep, ysend, coef_ref, cn_ref, scr, sems):
    copies = Copies(sems)
    share, cols = xkeep.shape[3:]
    coef_copy = copies.start(coef_hbm, coef_ref)
    cn_copies = [
        copies.start(cn_hbm.at[:, pl.ds(h * cols, cols)], cn_ref.at[h]) for h in range(2)
    ]
    x0, y0 = at_ref[0], at_ref[1]

    def rows(p, y, q, x):
        place = (2 * p + y) * NX + 2 * q + x
        return pl.ds(pl.multiple_of(place * share, share), share)

    out = []
    coef_copy.wait()
    coef = coef_ref[...]
    for h, (keep, send) in enumerate(((xkeep, xsend), (ykeep, ysend))):
        cn_copies[h].wait()
        scr[h] = lax.dot_general(
            coef, cn_ref[h], (((0,), (0,)), ((), ())), preferred_element_type=F32
        )
        for other in range(2):
            for p in range(NY // 2):
                for q in range(NX // 2):
                    if h == 0:
                        y = y0 if other == 0 else 1 - y0
                        mine, theirs = rows(p, y, q, x0), rows(p, y, q, 1 - x0)
                    else:
                        x = x0 if other == 0 else 1 - x0
                        mine, theirs = rows(p, y0, q, x), rows(p, 1 - y0, q, x)
                    out.append(copies.start(scr.at[h, theirs], send.at[other, p, q]))
                    out.append(copies.start(scr.at[h, mine], keep.at[other, p, q]))
    for copy in out:
        copy.wait()


def anchor_stage(at, coef, cn, share):
    m, width = cn.shape
    n = coef.shape[1]
    cols = width // 2
    part = jax.ShapeDtypeStruct((2, NY // 2, NX // 2, share, cols), F32)
    return pl.pallas_call(
        anchor_kernel,
        in_specs=[SMEM, HBM, HBM],
        out_specs=[HBM] * 4,
        out_shape=[part] * 4,
        scratch_shapes=[
            pltpu.VMEM((m, n), BF16),
            pltpu.VMEM((2, m, cols), BF16),
            pltpu.VMEM((2, n, cols), F32),
            pltpu.SemaphoreType.DMA((3 + 2 * NX * NY,)),
        ],
        compiler_params=pltpu.CompilerParams(vmem_limit_bytes=60 * MIB),
        cost_estimate=pl.CostEstimate(
            flops=2 * n * width * m, bytes_accessed=8 * MIB, transcendentals=0
        ),
        name="anchor_terms",
    )(at, coef, cn)


def probe_kernel(t_ref, a_ref, o_ref):
    term = jnp.sum(t_ref[...], axis=0)
    values = a_ref[...].astype(F32)
    inv = inverse_radius(values)
    unit = values * inv
    o_ref[...] = (term - unit * jnp.sum(unit * term, axis=1, keepdims=True)) * inv


def probe_stage(terms, rows):
    return pl.pallas_call(
        probe_kernel,
        out_shape=jax.ShapeDtypeStruct(rows.shape, F32),
        compiler_params=pltpu.CompilerParams(vmem_limit_bytes=8 * MIB),
        name="probe_derivatives",
    )(terms, rows)


def unpack_kernel(p_ref, o_ref):
    half = p_ref.shape[0]
    t = p_ref[...].T
    o_ref[:, :half] = t[: LANES // 2]
    o_ref[:, half:] = t[LANES // 2 :]


def unpack_stage(packed):
    half = packed.shape[0]
    return pl.pallas_call(
        unpack_kernel,
        out_shape=jax.ShapeDtypeStruct((LANES // 2, 2 * half), F32),
        compiler_params=pltpu.CompilerParams(vmem_limit_bytes=62 * MIB),
        name="unpack",
    )(packed)


def per_device(n_anc, anchors, candidates, anchor_group, cand_group, cotangent):
    n, width = anchors.shape
    n_cand = NX * NY
    share = n // n_cand
    anc, cand = lax.axis_index("anc"), lax.axis_index("cand")
    core = anc % 2
    y, x = cand // NX, cand % NX

    def swap(v, over_x):
        pairs = []
        for p in range(n_anc):
            for j in range(NY):
                for i in range(NX):
                    k = i if over_x else j
                    k += 1 if (k - p) % 2 == 0 else -1
                    to = j * NX + k % NX if over_x else (k % NY) * NX + i
                    pairs.append((p * n_cand + j * NX + i, p * n_cand + to))
        return lax.ppermute(v, ("anc", "cand"), pairs)

    ag, cg = anchor_group.reshape(1, n), cand_group.reshape(1, -1)
    an, cn, expo, st, row = score_stage(anchors, candidates, ag, cg, n_cand)
    st = lax.all_to_all(st, "cand", 0, 0, tiled=True)
    at = jnp.stack([x % 2, y % 2, core]).astype(jnp.int32)
    cost, coef, own, oth = candidate_stage(
        at, st, cotangent.reshape(1, n), ag, row, expo, an,
        candidates,
    )

    sibling = lax.ppermute(oth, "anc", [(p, p ^ 1) for p in range(n_anc)])
    parts = anchor_stage(at, coef.reshape(-1, n), cn, share)
    own, parts = lax.optimization_barrier((own, parts))
    both, parts = lax.optimization_barrier((own + sibling, parts))
    packed = lax.psum_scatter(
        both, "anc", scatter_dimension=0,
        axis_index_groups=[list(range(c, n_anc, 2)) for c in range(2)], tiled=False,
    )
    grad_candidates = unpack_stage(packed).T

    xkeep, xsend, ykeep, ysend = parts
    xgot, ygot = swap(xsend, True), swap(ysend, False)
    xagain, yagain = swap(xkeep[1] + xgot[1], False), swap(ykeep[1] + ygot[1], True)
    xpart, ypart = xkeep[0] + xgot[0] + xagain, ykeep[0] + ygot[0] + yagain
    groups = [
        [(2 * p + j) * NX + 2 * q + i for p in range(NY // 2) for q in range(NX // 2)]
        for j in range(2) for i in range(2)
    ]
    terms = jnp.concatenate([xpart, ypart], axis=-1).reshape(-1, share, width)
    terms = lax.all_to_all(terms, "cand", 0, 0, axis_index_groups=groups, tiled=True)
    rows = lax.dynamic_slice_in_dim(anchors, cand * share, share, 0)
    probe_derivatives = probe_stage(terms, rows)
    return cost.reshape(n), probe_derivatives, grad_candidates


def solution(mesh):
    in_specs = (P("anc", None), P("cand", None), P("anc"), P("cand"), P("anc"))
    out_specs = (P("anc"), P(("anc", "cand"), None), P("cand", "anc"))
    return jax.shard_map(
        functools.partial(per_device, mesh.shape["anc"]),
        mesh=mesh, in_specs=in_specs, out_specs=out_specs, check_vma=False,
    )
```

time: 139 us -> 134 us (0.964)
  the two profiles are of different devices: /device:TPU:1 before, /device:TPU:4 now
where the time goes in v2:
time: 134 us
  waiting for transfers between devices  55.4 us (41%)
  starting transfers between devices  31.6 us (24%)
  Pallas kernels  25.4 us (19%)
  between operations  14.2 us (11%)
  other arithmetic  5.63 us (4%)
  local copies, waits for them, and re-layouts  1.52 us (1%)
    all_to_all x1, waiting for transfers between devices, per_device(): lax.all_to_all(terms, 'cand', 0, 0, axis_index_groups=groups, tiled=True)  17.9 us
    ppermute x4, waiting for transfers between devices, swap(): return lax.ppermute(v, ('anc', 'cand'), pairs)  15.8 us
    all_to_all x1, starting transfers between devices, per_device(): st = lax.all_to_all(st, 'cand', 0, 0, tiled=True)  13.1 us
    reduce_scatter x1, waiting for transfers between devices, per_device(): lax.psum_scatter(both, 'anc', scatter_dimension=0, axis_index_groups=[lis...  12.4 us
    ppermute x4, starting transfers between devices, swap(): return lax.ppermute(v, ('anc', 'cand'), pairs)  10.8 us
    all_to_all x1, waiting for transfers between devices, per_device(): st = lax.all_to_all(st, 'cand', 0, 0, tiled=True)  9.2 us
    pallas_call x1, Pallas kernels, candidate_stage(): pl.pallas_call(candidate_kernel, in_specs=[SMEM, HBM, VMEM, VMEM, HBM, HB...  8.94 us
    pallas_call x1, Pallas kernels, score_stage(): pl.pallas_call(score_kernel, in_specs=[HBM, HBM, VMEM, VMEM], out_specs=[...  7.05 us
  transfers between devices with their start and end apart: 8, of which 7 were waited for; matrix products, arithmetic and copies ran while one was open for 2% of the time, Pallas kernels for 6%

profile of v2, /device:TPU:4, one launch (start us, length us, event | category | flops | bytes accessed | tf_op | source)
XLA Modules:
  0.0 133.8 jit_solution(6807914128437758251)
XLA Ops:
  7.2 7.0 %scores.1 = (bf16[512,1536]{1,0:T(8,128)(2,1)}, bf16[960,1536]{1,0:T(8,128)(2,1)}, f32[960,512]{1,0:T(8,128)}, f32[32,12,128]{2,1,0:T(8,128)}, f32[960,128]{1,0:T(8,128)}) custom-call(bf16[512,1536]{1,0:T(8,128)(2,1)} %a_hbm.1, bf16[960,1536]{1,0:T(8,128)(2,1)} %c_hbm.1, s32[1,512]{1,0:T(1,128)} %bitcast.31, s32[1,960]{1,0:T(1,128)} %bitcast.33), custom_call_target="tpu_custom_call" | custom-call | tf_op jit(solution)/shard_map/scores/pallas_call | solution.py:109
  14.2 13.1 %all-to-all-start = ((f32[32,12,128]{2,1,0:T(8,128)}), f32[32,12,128]{2,1,0:T(8,128)S(1)}, u32[]{:S(2)}, u32[]{:S(2)}) async-start(f32[32,12,128]{2,1,0:T(8,128)} %get-tuple-element.26), calls=%async_computation | async-start | bytes 524288 | tf_op jit(solution)/shard_map/all_to_all | solution.py:342
  27.4 0.6 pad_add_fusion.at_ref
  28.0 9.2 %all-to-all-done.st_hbm = f32[32,12,128]{2,1,0:T(8,128)S(1)} async-done(((f32[32,12,128]{2,1,0:T(8,128)}), f32[32,12,128]{2,1,0:T(8,128)S(1)}, u32[]{:S(2)}, u32[]{:S(2)}) %all-to-all-start) | async-done | bytes 196640 | tf_op jit(solution)/shard_map/all_to_all | solution.py:342
  37.2 0.7 copy-done.1
  37.9 8.9 %candidate_terms.1 = (f32[1,512]{1,0:T(1,128)}, bf16[2,480,512]{2,1,0:T(8,128)(2,1)}, f32[12,480,128]{2,1,0:T(8,128)}, f32[12,480,128]{2,1,0:T(8,128)}) custom-call(s32[3]{0:T(128)} %pad_add_fusion.at_ref, f32[32,12,128]{2,1,0:T(8,128)} %copy-done.1, f32[1,512]{1,0:T(1,128)} %bitcast.34, s32[1,512]{1,0:T(1,128)} %bitcast.32, f32[2,480,128]{2,1,0:T(8,128)} %bitcast.28, ...), custom_call_target="tpu_custom_call" | custom-call | tf_op jit(solution)/shard_map/candidate_terms/pallas_call | solution.py:210
  46.8 2.2 %collective-permute-start = (f32[12,480,128]{2,1,0:T(8,128)}, f32[12,480,128]{2,1,0:T(8,128)}, u32[]{:S(2)}, u32[]{:S(2)}) collective-permute-start(f32[12,480,128]{2,1,0:T(8,128)} %get-tuple-element.39), channel_id=1, source_target_pairs={{0,32},{32,0},{64,96},{96,64},{128,160},{160,128},{192,224},{224,1... | collective-permute-start | bytes 8847368 | tf_op jit(solution)/shard_map/ppermute | solution.py:349
  49.0 6.7 %anchor_terms.1 = (f32[2,4,2,16,768]{4,3,2,1,0:T(8,128)}, f32[2,4,2,16,768]{4,3,2,1,0:T(8,128)}, f32[2,4,2,16,768]{4,3,2,1,0:T(8,128)}, f32[2,4,2,16,768]{4,3,2,1,0:T(8,128)}) custom-call(s32[3]{0:T(128)} %pad_add_fusion.at_ref, bf16[960,512]{1,0:T(8,128)(2,1)} %bitcast.35, bf16[960,1536]{1,0:T(8,128)(2,1)} %get-tuple-element.33.cn_hbm), custom_call_target="tpu_custom_call" | custom-call | flops 1509949440 | bytes 8388608 | tf_op jit(solution)/shard_map/anchor_terms/pallas_call | solution.py:268
  55.8 3.8 %add.56 = f32[12,480,128]{2,1,0:T(8,128)} add(f32[12,480,128]{2,1,0:T(8,128)S(1)} %copy-done, f32[12,480,128]{2,1,0:T(8,128)} %collective-permute-done) | non-fusion elementwise | flops 737280 | bytes 8847360 | tf_op jit(solution)/shard_map/add | solution.py:352
  59.6 3.3 %collective-permute-start.1 = (f32[2,4,2,16,768]{4,3,2,1,0:T(8,128)S(1)}, f32[2,4,2,16,768]{4,3,2,1,0:T(8,128)S(1)}, u32[]{:S(2)}, u32[]{:S(2)}) collective-permute-start(f32[2,4,2,16,768]{4,3,2,1,0:T(8,128)S(1)} %copy-done.5), channel_id=1, source_target_pairs={{0,1},{1,0},{2,3},{3,2},{4,5},{5,4},{6,7},{7,6},{8,9},{9,8},{10,11... | collective-permute-start | bytes 2359304 | tf_op jit(solution)/shard_map/ppermute | solution.py:338
  62.9 2.5 %collective-permute-start.3 = (f32[2,4,2,16,768]{4,3,2,1,0:T(8,128)S(1)}, f32[2,4,2,16,768]{4,3,2,1,0:T(8,128)S(1)}, u32[]{:S(2)}, u32[]{:S(2)}) collective-permute-start(f32[2,4,2,16,768]{4,3,2,1,0:T(8,128)S(1)} %copy-done.4), channel_id=1, source_target_pairs={{0,4},{1,5},{2,6},{3,7},{4,0},{5,1},{6,2},{7,3},{8,12},{9,13},{10,... | collective-permute-start | bytes 2359304 | tf_op jit(solution)/shard_map/ppermute | solution.py:338
  65.5 8.2 %collective-permute-done.1 = f32[2,4,2,16,768]{4,3,2,1,0:T(8,128)S(1)} collective-permute-done((f32[2,4,2,16,768]{4,3,2,1,0:T(8,128)S(1)}, f32[2,4,2,16,768]{4,3,2,1,0:T(8,128)S(1)}, u32[]{:S(2)}, u32[]{:S(2)}) %collective-permute-start.1) | collective-permute-done | bytes 786464 | tf_op jit(solution)/shard_map/ppermute | solution.py:338
  73.7 2.3 %collective-permute-start.2 = (f32[4,2,16,768]{3,2,1,0:T(8,128)S(1)}, f32[4,2,16,768]{3,2,1,0:T(8,128)S(1)}, u32[]{:S(2)}, u32[]{:S(2)}) collective-permute-start(f32[4,2,16,768]{3,2,1,0:T(8,128)S(1)} %fusion.3), channel_id=1, source_target_pairs={{0,4},{1,5},{2,6},{3,7},{4,0},{5,1},{6,2},{7,3},{8,12},{9,13},{10,... | collective-permute-start | bytes 1179656 | tf_op jit(solution)/shard_map/ppermute | solution.py:338
  76.0 0.8 collective-permute-done.3
  76.9 2.7 %collective-permute-start.4 = (f32[4,2,16,768]{3,2,1,0:T(8,128)S(1)}, f32[4,2,16,768]{3,2,1,0:T(8,128)S(1)}, u32[]{:S(2)}, u32[]{:S(2)}) collective-permute-start(f32[4,2,16,768]{3,2,1,0:T(8,128)S(1)} %fusion), channel_id=1, source_target_pairs={{0,1},{1,0},{2,3},{3,2},{4,5},{5,4},{6,7},{7,6},{8,9},{9,8},{10,11... | collective-permute-start | bytes 1179656 | tf_op jit(solution)/shard_map/ppermute | solution.py:338
  79.6 3.8 %collective-permute-done.2 = f32[4,2,16,768]{3,2,1,0:T(8,128)S(1)} collective-permute-done((f32[4,2,16,768]{3,2,1,0:T(8,128)S(1)}, f32[4,2,16,768]{3,2,1,0:T(8,128)S(1)}, u32[]{:S(2)}, u32[]{:S(2)}) %collective-permute-start.2) | collective-permute-done | bytes 393248 | tf_op jit(solution)/shard_map/ppermute | solution.py:338
  83.4 3.1 %collective-permute-done.4 = f32[4,2,16,768]{3,2,1,0:T(8,128)S(1)} collective-permute-done((f32[4,2,16,768]{3,2,1,0:T(8,128)S(1)}, f32[4,2,16,768]{3,2,1,0:T(8,128)S(1)}, u32[]{:S(2)}, u32[]{:S(2)}) %collective-permute-start.4) | collective-permute-done | bytes 393248 | tf_op jit(solution)/shard_map/ppermute | solution.py:338
  86.6 1.0 pad_maximum_fusion
  87.6 5.5 %all-to-all-start.1 = ((f32[8,16,1536]{2,1,0:T(8,128)}), f32[8,16,1536]{2,1,0:T(8,128)S(1)}, u32[]{:S(2)}, u32[]{:S(2)}) async-start(f32[8,16,1536]{2,1,0:T(8,128)} %bitcast.15), calls=%async_computation.1 | async-start | bytes 1572864 | tf_op jit(solution)/shard_map/all_to_all | solution.py:368
  93.1 0.8 constant_dynamic-slice_fusion.a_ref
  93.9 17.9 %all-to-all-done.1.t_ref = f32[8,16,1536]{2,1,0:T(8,128)S(1)} async-done(((f32[8,16,1536]{2,1,0:T(8,128)}), f32[8,16,1536]{2,1,0:T(8,128)S(1)}, u32[]{:S(2)}, u32[]{:S(2)}) %all-to-all-start.1) | async-done | bytes 786464 | tf_op jit(solution)/shard_map/all_to_all | solution.py:368
  111.8 0.8 probe_derivatives.1
  112.7 12.4 %reduce-scatter.2.cloned.1.call-done = f32[1,480,128]{2,1,0:T(8,128)} async-done(((f32[12,480,128]{2,1,0:T(8,128)}), f32[1,480,128]{2,1,0:T(8,128)}) %reduce-scatter.2.cloned.1.call-update) | async-done | bytes 245776 | tf_op jit(solution)/shard_map/reduce_scatter | solution.py:353
  125.1 1.9 %unpack.1 = f32[64,960]{1,0:T(8,128)} custom-call(f32[480,128]{1,0:T(8,128)} %bitcast.30), custom_call_target="tpu_custom_call" | custom-call | tf_op jit(solution)/shard_map/unpack/pallas_call | solution.py:313
  (18 shorter events, 0.4 us)
Async XLA Ops:
  14.2 23.0 %all-to-all-start = ((f32[32,12,128]{2,1,0:T(8,128)}), f32[32,12,128]{2,1,0:T(8,128)S(1)}, u32[]{:S(2)}, u32[]{:S(2)}) async-start(f32[32,12,128]{2,1,0:T(8,128)} %get-tuple-element.26), calls=%async_computation | async-start | bytes 524288 | tf_op jit(solution)/shard_map/all_to_all | solution.py:342
  27.3 97.8 %reduce-scatter.2.cloned.1.call-start = ((), (), s32[]{:S(2)}) async-start(), calls=%async_computation.3 | async-start | bytes 3194880 | tf_op jit(solution)/shard_map/reduce_scatter | solution.py:353
  37.2 0.7 copy-start.1
  46.8 8.9 %copy-start = (f32[12,480,128]{2,1,0:T(8,128)S(1)}, f32[12,480,128]{2,1,0:T(8,128)}, u32[]{:S(2)}) copy-start(f32[12,480,128]{2,1,0:T(8,128)} %get-tuple-element.38) | copy-start | bytes 8847364
  46.8 8.9 %collective-permute-start = (f32[12,480,128]{2,1,0:T(8,128)}, f32[12,480,128]{2,1,0:T(8,128)}, u32[]{:S(2)}, u32[]{:S(2)}) collective-permute-start(f32[12,480,128]{2,1,0:T(8,128)} %get-tuple-element.39), channel_id=1, source_target_pairs={{0,32},{32,0},{64,96},{96,64},{128,160},{160,128},{192,224},{224,1... | collective-permute-start | bytes 8847368 | tf_op jit(solution)/shard_map/ppermute | solution.py:349
  55.8 3.8 %copy-start.5 = (f32[2,4,2,16,768]{4,3,2,1,0:T(8,128)S(1)}, f32[2,4,2,16,768]{4,3,2,1,0:T(8,128)}, u32[]{:S(2)}) copy-start(f32[2,4,2,16,768]{4,3,2,1,0:T(8,128)} %get-tuple-element.45) | copy-start | bytes 2359300
  59.6 3.3 %copy-start.4 = (f32[2,4,2,16,768]{4,3,2,1,0:T(8,128)S(1)}, f32[2,4,2,16,768]{4,3,2,1,0:T(8,128)}, u32[]{:S(2)}) copy-start(f32[2,4,2,16,768]{4,3,2,1,0:T(8,128)} %get-tuple-element.47) | copy-start | bytes 2359300
  59.6 14.1 %copy-start.3 = (f32[2,4,2,16,768]{4,3,2,1,0:T(8,128)S(1)}, f32[2,4,2,16,768]{4,3,2,1,0:T(8,128)}, u32[]{:S(2)}) copy-start(f32[2,4,2,16,768]{4,3,2,1,0:T(8,128)} %get-tuple-element.44) | copy-start | bytes 2359300
  59.6 17.2 %copy-start.2 = (f32[2,4,2,16,768]{4,3,2,1,0:T(8,128)S(1)}, f32[2,4,2,16,768]{4,3,2,1,0:T(8,128)}, u32[]{:S(2)}) copy-start(f32[2,4,2,16,768]{4,3,2,1,0:T(8,128)} %get-tuple-element.46) | copy-start | bytes 2359300
  59.6 14.0 %collective-permute-start.1 = (f32[2,4,2,16,768]{4,3,2,1,0:T(8,128)S(1)}, f32[2,4,2,16,768]{4,3,2,1,0:T(8,128)S(1)}, u32[]{:S(2)}, u32[]{:S(2)}) collective-permute-start(f32[2,4,2,16,768]{4,3,2,1,0:T(8,128)S(1)} %copy-done.5), channel_id=1, source_target_pairs={{0,1},{1,0},{2,3},{3,2},{4,5},{5,4},{6,7},{7,6},{8,9},{9,8},{10,11... | collective-permute-start | bytes 2359304 | tf_op jit(solution)/shard_map/ppermute | solution.py:338
  62.9 13.9 %collective-permute-start.3 = (f32[2,4,2,16,768]{4,3,2,1,0:T(8,128)S(1)}, f32[2,4,2,16,768]{4,3,2,1,0:T(8,128)S(1)}, u32[]{:S(2)}, u32[]{:S(2)}) collective-permute-start(f32[2,4,2,16,768]{4,3,2,1,0:T(8,128)S(1)} %copy-done.4), channel_id=1, source_target_pairs={{0,4},{1,5},{2,6},{3,7},{4,0},{5,1},{6,2},{7,3},{8,12},{9,13},{10,... | collective-permute-start | bytes 2359304 | tf_op jit(solution)/shard_map/ppermute | solution.py:338
  73.7 9.7 %collective-permute-start.2 = (f32[4,2,16,768]{3,2,1,0:T(8,128)S(1)}, f32[4,2,16,768]{3,2,1,0:T(8,128)S(1)}, u32[]{:S(2)}, u32[]{:S(2)}) collective-permute-start(f32[4,2,16,768]{3,2,1,0:T(8,128)S(1)} %fusion.3), channel_id=1, source_target_pairs={{0,4},{1,5},{2,6},{3,7},{4,0},{5,1},{6,2},{7,3},{8,12},{9,13},{10,... | collective-permute-start | bytes 1179656 | tf_op jit(solution)/shard_map/ppermute | solution.py:338
  76.9 9.7 %collective-permute-start.4 = (f32[4,2,16,768]{3,2,1,0:T(8,128)S(1)}, f32[4,2,16,768]{3,2,1,0:T(8,128)S(1)}, u32[]{:S(2)}, u32[]{:S(2)}) collective-permute-start(f32[4,2,16,768]{3,2,1,0:T(8,128)S(1)} %fusion), channel_id=1, source_target_pairs={{0,1},{1,0},{2,3},{3,2},{4,5},{5,4},{6,7},{7,6},{8,9},{9,8},{10,11... | collective-permute-start | bytes 1179656 | tf_op jit(solution)/shard_map/ppermute | solution.py:338
  87.6 24.2 %all-to-all-start.1 = ((f32[8,16,1536]{2,1,0:T(8,128)}), f32[8,16,1536]{2,1,0:T(8,128)S(1)}, u32[]{:S(2)}, u32[]{:S(2)}) async-start(f32[8,16,1536]{2,1,0:T(8,128)} %bitcast.15), calls=%async_computation.1 | async-start | bytes 1572864 | tf_op jit(solution)/shard_map/all_to_all | solution.py:368
Sparse Core Ops, SparseCore 0:
  59.7 65.3 reduce-scatter.1

commit v3 on v2

v3 whole, which is shorter than its diff:
```python
import functools

import jax
import jax.numpy as jnp
from jax import lax
from jax.experimental import pallas as pl
from jax.experimental.pallas import tpu as pltpu
from jax.sharding import PartitionSpec as P

SCALE = 20.0
EPS = 1e-06
F32 = jnp.float32
BF16 = jnp.bfloat16
NX, NY = 4, 8
LANES = 128
SLOTS = 12
SPARE = 8
MIB = 2**20
VMEM = pl.BlockSpec(memory_space=pltpu.VMEM)
HBM = pl.BlockSpec(memory_space=pltpu.HBM)
SMEM = pl.BlockSpec(memory_space=pltpu.SMEM)


def inverse_radius(values):
    return 1.0 / jnp.sqrt(jnp.sum(values * values, axis=1, keepdims=True) + EPS)


class Copies:
    def __init__(self, sems):
        self.sems, self.all = sems, []

    def start(self, source, target):
        copy = pltpu.make_async_copy(source, target, self.sems.at[len(self.all)])
        copy.start()
        self.all.append(copy)
        return copy


def core_columns(values, core):
    side = (lax.broadcasted_iota(jnp.int32, (values.shape[0], LANES), 1) >= LANES // 2).astype(jnp.int32)
    stay = side == core
    blocks = []
    for k in range(0, values.shape[1], 2 * LANES):
        left, right = values[:, k : k + LANES], values[:, k + LANES : k + 2 * LANES]
        kept = jnp.where(core == 0, left, right)
        moved = jnp.where(core == 0, right, left)
        blocks.append(jnp.where(stay, kept, pltpu.roll(moved, LANES // 2, 1)))
    return blocks


SCORE_STEPS = 4
SCORE_COPIES = 4 + 4 * SCORE_STEPS


def score_kernel(
    a_hbm, c_hbm, ag_ref, cg_ref, cot_ref, an_hbm, x_hbm, st_hbm, row_hbm, cc_hbm,
    a_ref, c_ref, full_ref, an_ref, x_ref, st_ref, row_ref, cc_ref, acc_ref, sems,
):
    n, m = a_ref.shape[0], c_ref.shape[0]
    per = n // LANES
    core = lax.axis_index("anc") % 2
    rows = m // SCORE_STEPS
    parts = [pl.ds(k * rows, rows) for k in range(SCORE_STEPS)]
    copies = Copies(sems)
    a_copy = copies.start(a_hbm, a_ref)
    c_copies = [copies.start(c_hbm.at[part], c_ref.at[part]) for part in parts]
    out = []
    for k in range(0, m, LANES):
        size = min(LANES, m - k)
        row_ref[k : k + size, :] = jnp.broadcast_to(
            cg_ref[:, k : k + size].astype(F32), (LANES, size)
        ).T
    ag = ag_ref[...].astype(F32)
    x_ref[m + n : m + n + SPARE, :] = jnp.zeros((SPARE, n), F32)
    x_ref[m + n : m + n + 1, :] = ag
    x_ref[m + n + 1 : m + n + 2, :] = cot_ref[...]
    a_copy.wait()
    for r in range(0, n, LANES):
        values = a_ref[r : r + LANES, :].astype(F32)
        unit = values * inverse_radius(values)
        full_ref[r : r + LANES, :] = unit.astype(BF16)
        for k, block in enumerate(core_columns(unit, core)):
            an_ref[r : r + LANES, k * LANES : (k + 1) * LANES] = block.astype(BF16)
        for k, block in enumerate(core_columns(unit, 1 - core)):
            first = m + r if k < per else m + n + SPARE + r
            k = k % per
            x_ref[first : first + LANES, k * LANES : (k + 1) * LANES] = block
    rest = pl.ds(m, x_ref.shape[0] - m)
    out.append(copies.start(x_ref.at[rest], x_hbm.at[rest]))
    out.append(copies.start(an_ref, an_hbm))
    left = lax.broadcasted_iota(jnp.int32, (rows, LANES), 1) < LANES // 2
    acc = None
    for part, c_copy in zip(parts, c_copies):
        c_copy.wait()
        values = c_ref[part, :].astype(F32)
        inv = inverse_radius(values)
        scores = SCALE * lax.dot_general(
            (values * inv).astype(BF16), full_ref[...], (((1,), (1,)), ((), ())),
            preferred_element_type=F32,
        )
        expo = jnp.exp(scores - SCALE)
        x_ref[part, :] = expo
        out.append(copies.start(x_ref.at[part], x_hbm.at[part]))
        group = row_ref[part, :]
        row_ref[part, :] = jnp.where(left, inv, group)
        out.append(copies.start(row_ref.at[part], row_hbm.at[part]))
        for k, block in enumerate(core_columns(values, core)):
            cc_ref[part, k * LANES : (k + 1) * LANES] = block.astype(BF16)
        out.append(copies.start(cc_ref.at[part], cc_hbm.at[part]))
        match = group[:, LANES - 1 :] == ag
        sums = (
            jnp.sum(expo, axis=0, keepdims=True),
            jnp.sum(jnp.where(match, 1.0, 0.0), axis=0, keepdims=True),
            jnp.sum(jnp.where(match, scores, 0.0), axis=0, keepdims=True),
        )
        acc = sums if acc is None else tuple(u + v for u, v in zip(acc, sums))
    for k, s in enumerate(acc):
        for j in range(per):
            acc_ref[k * per + j : k * per + j + 1, :] = s[:, j * LANES : (j + 1) * LANES]
    st_ref[...] = jnp.broadcast_to(acc_ref[...][None], st_ref.shape)
    out.append(copies.start(st_ref, st_hbm))
    for copy in out:
        copy.wait()


def score_stage(anchors, candidates, ag, cg, cot, copies):
    n, width = anchors.shape
    m = candidates.shape[0]
    shapes = [
        ((n, width // 2), BF16),
        ((m + 2 * n + SPARE, n), F32),
        ((copies, SLOTS, LANES), F32),
        ((m, LANES), F32),
        ((m, width // 2), BF16),
    ]
    return pl.pallas_call(
        score_kernel,
        in_specs=[HBM, HBM, VMEM, VMEM, VMEM],
        out_specs=[HBM] * 5,
        out_shape=[jax.ShapeDtypeStruct(*s) for s in shapes],
        scratch_shapes=[
            pltpu.VMEM((n, width), BF16),
            pltpu.VMEM((m, width), BF16),
            pltpu.VMEM((n, width), BF16),
            *(pltpu.VMEM(*s) for s in shapes),
            pltpu.VMEM((SLOTS, LANES), F32),
            pltpu.SemaphoreType.DMA((SCORE_COPIES,)),
        ],
        compiler_params=pltpu.CompilerParams(vmem_limit_bytes=62 * MIB),
        name="scores",
    )(anchors, candidates, ag, cg, cot)


CANDIDATE_STEPS = 3
CANDIDATE_COPIES = 3 + 6 * CANDIDATE_STEPS


def candidate_kernel(
    st_ref, other_ref, cot_ref, ag_ref, row_hbm, cc_hbm, an_hbm, x_hbm, y_hbm,
    cost_ref, coef_hbm, own_hbm,
    row_ref, cc_ref, x_ref, y_ref, an_ref, extra_ref, more_ref, coef_ref, own_ref, sems,
):
    n = ag_ref.shape[1]
    half = own_ref.shape[1]
    m = 2 * half
    rows = half // CANDIDATE_STEPS
    per = n // LANES
    wide = more_ref.shape[1]
    parts = [pl.ds(k * rows, rows) for k in range(CANDIDATE_STEPS)]
    copies = Copies(sems)
    extra_copy = copies.start(y_hbm.at[pl.ds(m, n + SPARE)], extra_ref)
    more_copy = copies.start(
        y_hbm.at[pl.ds(m + n + SPARE, n), pl.ds(0, wide)], more_ref
    )
    an_copy = copies.start(an_hbm, an_ref.at[pl.ds(0, n)])
    ready = []
    for part in parts:
        ready.append([copies.start(row_hbm.at[:, part], row_ref.at[:, part])])
        for side in range(2):
            place = pl.ds(side * half + part.start, rows)
            ready[-1].append(copies.start(x_hbm.at[place], x_ref.at[side, part]))
            ready[-1].append(copies.start(y_hbm.at[place], y_ref.at[side, part]))
        ready[-1].append(copies.start(cc_hbm.at[:, part], cc_ref.at[:, part]))
    out = []

    def sums(ref):
        st = ref[...]
        total, count, positive = (
            jnp.concatenate([st[k * per + j : k * per + j + 1, :] for j in range(per)], axis=1)
            for k in range(3)
        )
        return total, jnp.maximum(count, 1.0), positive

    total, count, positive = sums(st_ref)
    cost_ref[...] = SCALE + jnp.log(total) - positive / count
    extra_copy.wait()
    factors = [(SCALE * cot_ref[...], 1.0 / total, 1.0 / count, ag_ref[...].astype(F32))]
    total, count, _ = sums(other_ref)
    factors.append((SCALE * extra_ref[n + 1 : n + 2, :], 1.0 / total, 1.0 / count, extra_ref[n : n + 1, :]))
    an_ref[n:, :n] = extra_ref[:n, :].astype(BF16)
    more_copy.wait()
    an_ref[n:, n:] = more_ref[...].astype(BF16)
    low = lax.broadcasted_iota(jnp.int32, (rows, LANES), 1) < LANES // 2

    def coefficients(ref, side, part, factor):
        cot, per_total, per_count, ag = factor
        match = row_ref[side, part, LANES - 1 :] == ag
        expo = ref[side, part, :]
        coef = (cot * (expo * per_total - jnp.where(match, per_count, 0.0))).astype(BF16)
        cosine = 1.0 + jnp.log(expo) * (1.0 / SCALE)
        return coef, jnp.sum(coef.astype(F32) * cosine, axis=1, keepdims=True)

    for k, part in enumerate(parts):
        for copy in ready[k]:
            copy.wait()
        coefs = []
        for side in range(2):
            mine, inner = coefficients(x_ref, side, part, factors[0])
            theirs, more = coefficients(y_ref, side, part, factors[1])
            coef_ref[side, part, :] = mine
            coefs.append((jnp.concatenate([mine, theirs], axis=1), inner + more))
        out.append(copies.start(coef_ref.at[:, part], coef_hbm.at[:, part]))
        if k == 0:
            an_copy.wait()
        grads = []
        for side, (coef, inner) in enumerate(coefs):
            dcn = jnp.dot(coef, an_ref[...], preferred_element_type=F32)
            inv = row_ref[side, part, :1]
            grads.append(inv * (dcn - cc_ref[side, part, :].astype(F32) * (inv * inner)))
        over, under = grads
        for b in range(own_ref.shape[0] // 2):
            top = over[:, b * LANES : (b + 1) * LANES]
            bottom = under[:, b * LANES : (b + 1) * LANES]
            own_ref[2 * b, part, :] = jnp.where(low, top, pltpu.roll(bottom, LANES // 2, 1))
            own_ref[2 * b + 1, part, :] = jnp.where(low, pltpu.roll(top, LANES // 2, 1), bottom)
        out.append(copies.start(own_ref.at[:, part], own_hbm.at[:, part]))
    for copy in out:
        copy.wait()


def candidate_stage(st, other, cot, ag, row, cc, an, x, y):
    n, cols = an.shape
    half = row.shape[0] // 2
    split = lambda v: v.reshape(2, half, -1)
    outs = [((2, half, n), BF16), ((2 * cols // LANES, half, LANES), F32)]
    scratch = [
        ((2, half, LANES), F32),
        ((2, half, cols), BF16),
        ((2, half, n), F32),
        ((2, half, n), F32),
        ((2 * n, cols), BF16),
        ((n + SPARE, n), F32),
        ((n, cols - n), F32),
    ]
    return pl.pallas_call(
        candidate_kernel,
        in_specs=[VMEM] * 4 + [HBM] * 5,
        out_specs=[VMEM, HBM, HBM],
        out_shape=[jax.ShapeDtypeStruct(*s) for s in [((1, n), F32)] + outs],
        scratch_shapes=[
            *(pltpu.VMEM(*s) for s in scratch + outs),
            pltpu.SemaphoreType.DMA((CANDIDATE_COPIES + 2 * CANDIDATE_STEPS,)),
        ],
        compiler_params=pltpu.CompilerParams(vmem_limit_bytes=60 * MIB),
        name="candidate_terms",
    )(st, other, cot, ag, split(row), split(cc), an, x, y)


def anchor_kernel(
    coef_hbm, row_hbm, c_hbm, xkeep, xsend, ykeep, ysend, coef_ref, row_ref, c_ref, scr, sems,
):
    copies = Copies(sems)
    share, cols = xkeep.shape[3:]
    row_copy = copies.start(row_hbm, row_ref)
    c_copies = [copies.start(c_hbm.at[:, pl.ds(h * cols, cols)], c_ref.at[h]) for h in range(2)]
    coef_copy = copies.start(coef_hbm, coef_ref)
    cand = lax.axis_index("cand")
    x0, y0 = cand % 2, (cand // NX) % 2

    out = []
    row_copy.wait()
    inv = row_ref[:, :1]
    for h, (keep, send) in enumerate(((xkeep, xsend), (ykeep, ysend))):
        c_copies[h].wait()
        cn = (c_ref[h].astype(F32) * inv).astype(BF16)
        if h == 0:
            coef_copy.wait()
        scr[h] = lax.dot_general(
            coef_ref[...], cn, (((0,), (0,)), ((), ())), preferred_element_type=F32
        ).reshape(scr.shape[1:])
        for other in range(2):
            if h == 0:
                y = y0 if other == 0 else 1 - y0
                mine, theirs = (y, x0), (y, 1 - x0)
            else:
                x = x0 if other == 0 else 1 - x0
                mine, theirs = (y0, x), (1 - y0, x)
            for (j, i), to in ((theirs, send), (mine, keep)):
                out.append(copies.start(scr.at[h, :, j, :, i], to.at[other]))
    for copy in out:
        copy.wait()


def anchor_stage(coef, row, candidates, share):
    m, width = candidates.shape
    n = coef.shape[1]
    cols = width // 2
    part = jax.ShapeDtypeStruct((2, NY // 2, NX // 2, share, cols), F32)
    return pl.pallas_call(
        anchor_kernel,
        in_specs=[HBM, HBM, HBM],
        out_specs=[HBM] * 4,
        out_shape=[part] * 4,
        scratch_shapes=[
            pltpu.VMEM((m, n), BF16),
            pltpu.VMEM((m, LANES), F32),
            pltpu.VMEM((2, m, cols), BF16),
            pltpu.VMEM((2, NY // 2, 2, NX // 2, 2, share, cols), F32),
            pltpu.SemaphoreType.DMA((12,)),
        ],
        compiler_params=pltpu.CompilerParams(vmem_limit_bytes=60 * MIB),
        cost_estimate=pl.CostEstimate(
            flops=2 * n * width * m, bytes_accessed=8 * MIB, transcendentals=0
        ),
        name="anchor_terms",
    )(coef, row, candidates)


def probe_kernel(t_ref, a_ref, o_ref):
    term = jnp.sum(t_ref[...], axis=0)
    values = a_ref[...].astype(F32)
    inv = inverse_radius(values)
    unit = values * inv
    o_ref[...] = (term - unit * jnp.sum(unit * term, axis=1, keepdims=True)) * inv


def probe_stage(terms, rows):
    return pl.pallas_call(
        probe_kernel,
        out_shape=jax.ShapeDtypeStruct(rows.shape, F32),
        compiler_params=pltpu.CompilerParams(vmem_limit_bytes=8 * MIB),
        name="probe_derivatives",
    )(terms, rows)


def unpack_kernel(p_ref, o_ref):
    half = p_ref.shape[0]
    t = p_ref[...].T
    o_ref[:, :half] = t[: LANES // 2]
    o_ref[:, half:] = t[LANES // 2 :]


def unpack_stage(packed):
    half = packed.shape[0]
    return pl.pallas_call(
        unpack_kernel,
        out_shape=jax.ShapeDtypeStruct((LANES // 2, 2 * half), F32),
        compiler_params=pltpu.CompilerParams(vmem_limit_bytes=62 * MIB),
        name="unpack",
    )(packed)


def per_device(n_anc, anchors, candidates, anchor_group, cand_group, cotangent):
    n, width = anchors.shape
    n_cand = NX * NY
    share = n // n_cand
    cand = lax.axis_index("cand")

    def swap(v, over_x):
        pairs = []
        for p in range(n_anc):
            for j in range(NY):
                for i in range(NX):
                    k = i if over_x else j
                    k += 1 if (k - p) % 2 == 0 else -1
                    to = j * NX + k % NX if over_x else (k % NY) * NX + i
                    pairs.append((p * n_cand + j * NX + i, p * n_cand + to))
        return lax.ppermute(v, ("anc", "cand"), pairs)

    def sibling(v):
        return lax.ppermute(v, "anc", [(p, p ^ 1) for p in range(n_anc)])

    ag, cg, cot = anchor_group.reshape(1, n), cand_group.reshape(1, -1), cotangent.reshape(1, n)
    an, mine, st, row, cc = score_stage(anchors, candidates, ag, cg, cot, n_cand)

    theirs = sibling(mine)
    st = jnp.sum(lax.all_to_all(st, "cand", 0, 0, tiled=True), axis=0)
    cost, coef, packed = candidate_stage(st, sibling(st), cot, ag, row, cc, an, mine, theirs)
    packed = lax.psum_scatter(
        packed, "anc", scatter_dimension=0,
        axis_index_groups=[list(range(c, n_anc, 2)) for c in range(2)], tiled=False,
    )
    grad_candidates = unpack_stage(packed).T

    xkeep, xsend, ykeep, ysend = anchor_stage(coef.reshape(-1, n), row, candidates, share)
    xgot, ygot = swap(xsend, True), swap(ysend, False)
    xagain, yagain = swap(xkeep[1] + xgot[1], False), swap(ykeep[1] + ygot[1], True)
    xpart, ypart = xkeep[0] + xgot[0] + xagain, ykeep[0] + ygot[0] + yagain
    groups = [
        [(2 * p + j) * NX + 2 * q + i for p in range(NY // 2) for q in range(NX // 2)]
        for j in range(2) for i in range(2)
    ]
    terms = jnp.concatenate([xpart, ypart], axis=-1).reshape(-1, share, width)
    terms = lax.all_to_all(terms, "cand", 0, 0, axis_index_groups=groups, tiled=True)
    rows = lax.dynamic_slice_in_dim(anchors, cand * share, share, 0)
    probe_derivatives = probe_stage(terms, rows)
    return cost.reshape(n), probe_derivatives, grad_candidates


def solution(mesh):
    in_specs = (P("anc", None), P("cand", None), P("anc"), P("cand"), P("anc"))
    out_specs = (P("anc"), P(("anc", "cand"), None), P("cand", "anc"))
    return jax.shard_map(
        functools.partial(per_device, mesh.shape["anc"]),
        mesh=mesh, in_specs=in_specs, out_specs=out_specs, check_vma=False,
    )
```

time: 134 us -> 131 us (0.978)
  the two profiles are of different devices: /device:TPU:4 before, /device:TPU:1 now
where the time goes in v3:
time: 131 us; the launch traced here: 130 us
  waiting for transfers between devices  37.9 us (29%)
  starting transfers between devices  30.8 us (24%)
  Pallas kernels  25.6 us (20%)
  blocking collectives  16 us (12%)
  between operations  14.1 us (11%)
  other arithmetic  4.25 us (3%)
  local copies, waits for them, and re-layouts  1.4 us (1%)
    all_to_all x1, waiting for transfers between devices, per_device(): lax.all_to_all(terms, 'cand', 0, 0, axis_index_groups=groups, tiled=True)  21.8 us
    ppermute x2, starting transfers between devices, sibling(): return lax.ppermute(v, 'anc', [(p, p ^ 1) for p in range(n_anc)])  16.1 us
    all_to_all x1, blocking collectives, per_device(): st = jnp.sum(lax.all_to_all(st, 'cand', 0, 0, tiled=True), axis=0)  16 us
    ppermute x4, waiting for transfers between devices, swap(): return lax.ppermute(v, ('anc', 'cand'), pairs)  15.3 us
    ppermute x4, starting transfers between devices, swap(): return lax.ppermute(v, ('anc', 'cand'), pairs)  9.99 us
    pallas_call x1, Pallas kernels, candidate_stage(): pl.pallas_call(candidate_kernel, in_specs=[VMEM] * 4 + [HBM] * 5, out_spe...  8.61 us
    pallas_call x1, Pallas kernels, score_stage(): pl.pallas_call(score_kernel, in_specs=[HBM, HBM, VMEM, VMEM, VMEM], out_s...  8.19 us
    pallas_call x1, Pallas kernels, anchor_stage(): pl.pallas_call(anchor_kernel, in_specs=[HBM, HBM, HBM], out_specs=[HBM] *...  6.08 us
  transfers between devices with their start and end apart: 8, of which 5 were waited for; matrix products, arithmetic and copies ran while one was open for 4% of the time, Pallas kernels for 5%

profile of v3, /device:TPU:1, one launch (start us, length us, event | category | flops | bytes accessed | tf_op | source)
XLA Modules:
  0.0 130.1 jit_solution(13998619600061181593)
XLA Ops:
  7.2 8.2 %scores.1 = (bf16[512,768]{1,0:T(8,128)(2,1)}, f32[1992,512]{1,0:T(8,128)}, f32[32,12,128]{2,1,0:T(8,128)}, f32[960,128]{1,0:T(8,128)}, bf16[960,768]{1,0:T(8,128)(2,1)}) custom-call(bf16[512,1536]{1,0:T(8,128)(2,1)} %a_hbm.1, bf16[960,1536]{1,0:T(8,128)(2,1)} %c_hbm.3, s32[1,512]{1,0:T(1,128)} %bitcast.26, s32[1,960]{1,0:T(1,128)} %bitcast.30, ...), custom_call_target="tpu_custom_call" | custom-call | tf_op jit(solution)/shard_map/scores/pallas_call | solution.py:136
  15.4 12.4 %collective-permute-start.1 = (f32[1992,512]{1,0:T(8,128)}, f32[1992,512]{1,0:T(8,128)}, u32[]{:S(2)}, u32[]{:S(2)}) collective-permute-start(f32[1992,512]{1,0:T(8,128)} %get-tuple-element.19.x_hbm), channel_id=1, source_target_pairs={{0,32},{32,0},{64,96},{96,64},{128,160},{160,128},{192,224},{224,1... | collective-permute-start | bytes 12238856 | tf_op jit(solution)/shard_map/ppermute | solution.py:381
  27.8 16.0 %all_to_all.10 = f32[32,12,128]{2,1,0:T(8,128)S(1)} all-to-all(f32[32,12,128]{2,1,0:T(8,128)} %get-tuple-element.15), channel_id=1, replica_groups=mesh['anc'=24,'cand'=32] {'cand'}, dimensions={0} | all-to-all | bytes 393216 | tf_op jit(solution)/shard_map/all_to_all | solution.py:387
  43.9 3.6 %collective-permute-start = (f32[12,128]{1,0:T(8,128)S(1)}, f32[12,128]{1,0:T(8,128)S(1)}, u32[]{:S(2)}, u32[]{:S(2)}) collective-permute-start(f32[12,128]{1,0:T(8,128)S(1)} %reduce_sum.9.st_ref), channel_id=1, source_target_pairs={{0,32},{32,0},{64,96},{96,64},{128,160},{160,128},{192,224},{224,1... | collective-permute-start | bytes 18440 | tf_op jit(solution)/shard_map/ppermute | solution.py:381
  47.6 0.8 collective-permute-done.other_ref
  48.4 0.6 copy-done.2
  49.0 8.6 %candidate_terms.1 = (f32[1,512]{1,0:T(1,128)}, bf16[2,480,512]{2,1,0:T(8,128)(2,1)}, f32[12,480,128]{2,1,0:T(8,128)}) custom-call(f32[12,128]{1,0:T(8,128)} %copy-done.1, f32[12,128]{1,0:T(8,128)} %copy-done.2, f32[1,512]{1,0:T(1,128)} %bitcast.29, s32[1,512]{1,0:T(1,128)} %bitcast.27, f32[2,480,128]{2,1,0:T(8,128)} %bitcast.23, ...), custom_call_target="tpu_custom_call" | custom-call | tf_op jit(solution)/shard_map/candidate_terms/pallas_call | solution.py:255
  57.6 6.1 %anchor_terms.1 = (f32[2,4,2,16,768]{4,3,2,1,0:T(8,128)}, f32[2,4,2,16,768]{4,3,2,1,0:T(8,128)}, f32[2,4,2,16,768]{4,3,2,1,0:T(8,128)}, f32[2,4,2,16,768]{4,3,2,1,0:T(8,128)}) custom-call(bf16[960,512]{1,0:T(8,128)(2,1)} %bitcast.31, f32[960,128]{1,0:T(8,128)} %get-tuple-element.16.row_hbm, bf16[960,1536]{1,0:T(8,128)(2,1)} %c_hbm.3), custom_call_target="tpu_custom_call" | custom-call | flops 1509949440 | bytes 8388608 | tf_op jit(solution)/shard_map/anchor_terms/pallas_call | solution.py:309
  63.7 3.0 %collective-permute-start.2 = (f32[2,4,2,16,768]{4,3,2,1,0:T(8,128)}, f32[2,4,2,16,768]{4,3,2,1,0:T(8,128)S(1)}, u32[]{:S(2)}, u32[]{:S(2)}) collective-permute-start(f32[2,4,2,16,768]{4,3,2,1,0:T(8,128)} %get-tuple-element.23), channel_id=1, source_target_pairs={{0,1},{1,0},{2,3},{3,2},{4,5},{5,4},{6,7},{7,6},{8,9},{9,8},{10,11... | collective-permute-start | bytes 2359304 | tf_op jit(solution)/shard_map/ppermute | solution.py:378
  66.7 1.9 %collective-permute-start.4 = (f32[2,4,2,16,768]{4,3,2,1,0:T(8,128)}, f32[2,4,2,16,768]{4,3,2,1,0:T(8,128)S(1)}, u32[]{:S(2)}, u32[]{:S(2)}) collective-permute-start(f32[2,4,2,16,768]{4,3,2,1,0:T(8,128)} %get-tuple-element.25), channel_id=1, source_target_pairs={{0,4},{1,5},{2,6},{3,7},{4,0},{5,1},{6,2},{7,3},{8,12},{9,13},{10,... | collective-permute-start | bytes 2359304 | tf_op jit(solution)/shard_map/ppermute | solution.py:378
  68.7 9.7 %collective-permute-done.2 = f32[2,4,2,16,768]{4,3,2,1,0:T(8,128)S(1)} collective-permute-done((f32[2,4,2,16,768]{4,3,2,1,0:T(8,128)}, f32[2,4,2,16,768]{4,3,2,1,0:T(8,128)S(1)}, u32[]{:S(2)}, u32[]{:S(2)}) %collective-permute-start.2) | collective-permute-done | bytes 786464 | tf_op jit(solution)/shard_map/ppermute | solution.py:378
  78.4 1.0 fusion.3
  79.4 1.9 %collective-permute-start.3 = (f32[4,2,16,768]{3,2,1,0:T(8,128)S(1)}, f32[4,2,16,768]{3,2,1,0:T(8,128)S(1)}, u32[]{:S(2)}, u32[]{:S(2)}) collective-permute-start(f32[4,2,16,768]{3,2,1,0:T(8,128)S(1)} %fusion.3), channel_id=1, source_target_pairs={{0,4},{1,5},{2,6},{3,7},{4,0},{5,1},{6,2},{7,3},{8,12},{9,13},{10,... | collective-permute-start | bytes 1179656 | tf_op jit(solution)/shard_map/ppermute | solution.py:378
  81.4 1.1 fusion
  82.4 3.1 %collective-permute-start.5 = (f32[4,2,16,768]{3,2,1,0:T(8,128)S(1)}, f32[4,2,16,768]{3,2,1,0:T(8,128)S(1)}, u32[]{:S(2)}, u32[]{:S(2)}) collective-permute-start(f32[4,2,16,768]{3,2,1,0:T(8,128)S(1)} %fusion), channel_id=1, source_target_pairs={{0,1},{1,0},{2,3},{3,2},{4,5},{5,4},{6,7},{7,6},{8,9},{9,8},{10,11... | collective-permute-start | bytes 1179656 | tf_op jit(solution)/shard_map/ppermute | solution.py:378
  85.6 4.0 %collective-permute-done.3 = f32[4,2,16,768]{3,2,1,0:T(8,128)S(1)} collective-permute-done((f32[4,2,16,768]{3,2,1,0:T(8,128)S(1)}, f32[4,2,16,768]{3,2,1,0:T(8,128)S(1)}, u32[]{:S(2)}, u32[]{:S(2)}) %collective-permute-start.3) | collective-permute-done | bytes 393248 | tf_op jit(solution)/shard_map/ppermute | solution.py:378
  89.6 1.1 fusion.5
  90.6 1.5 %collective-permute-done.5 = f32[4,2,16,768]{3,2,1,0:T(8,128)S(1)} collective-permute-done((f32[4,2,16,768]{3,2,1,0:T(8,128)S(1)}, f32[4,2,16,768]{3,2,1,0:T(8,128)S(1)}, u32[]{:S(2)}, u32[]{:S(2)}) %collective-permute-start.5) | collective-permute-done | bytes 393248 | tf_op jit(solution)/shard_map/ppermute | solution.py:378
  92.3 1.0 pad_maximum_fusion
  93.2 4.7 %all-to-all-start.1 = ((f32[8,16,1536]{2,1,0:T(8,128)}), f32[8,16,1536]{2,1,0:T(8,128)S(1)}, u32[]{:S(2)}, u32[]{:S(2)}) async-start(f32[8,16,1536]{2,1,0:T(8,128)} %bitcast.11), calls=%async_computation.1 | async-start | bytes 1572864 | tf_op jit(solution)/shard_map/all_to_all | solution.py:404
  97.9 0.8 constant_dynamic-slice_fusion.a_ref
  98.7 21.8 %all-to-all-done.1.t_ref = f32[8,16,1536]{2,1,0:T(8,128)S(1)} async-done(((f32[8,16,1536]{2,1,0:T(8,128)}), f32[8,16,1536]{2,1,0:T(8,128)S(1)}, u32[]{:S(2)}, u32[]{:S(2)}) %all-to-all-start.1) | async-done | bytes 786464 | tf_op jit(solution)/shard_map/all_to_all | solution.py:404
  120.6 0.8 probe_derivatives.1
  121.4 1.9 %unpack.1 = f32[64,960]{1,0:T(8,128)} custom-call(f32[480,128]{1,0:T(8,128)} %bitcast.25), custom_call_target="tpu_custom_call" | custom-call | tf_op jit(solution)/shard_map/unpack/pallas_call | solution.py:355
  (12 shorter events, 0.2 us)
Async XLA Ops:
  7.2 114.3 %reduce-scatter.2.cloned.1.call-start = ((), (), s32[]{:S(2)}) async-start(), calls=%async_computation.3 | async-start | bytes 3194880 | tf_op jit(solution)/shard_map/reduce_scatter | solution.py:389
  15.4 33.0 %collective-permute-start.1 = (f32[1992,512]{1,0:T(8,128)}, f32[1992,512]{1,0:T(8,128)}, u32[]{:S(2)}, u32[]{:S(2)}) collective-permute-start(f32[1992,512]{1,0:T(8,128)} %get-tuple-element.19.x_hbm), channel_id=1, source_target_pairs={{0,32},{32,0},{64,96},{96,64},{128,160},{160,128},{192,224},{224,1... | collective-permute-start | bytes 12238856 | tf_op jit(solution)/shard_map/ppermute | solution.py:381
  43.9 4.5 %copy-start.1 = (f32[12,128]{1,0:T(8,128)}, f32[12,128]{1,0:T(8,128)S(1)}, u32[]{:S(2)}) copy-start(f32[12,128]{1,0:T(8,128)S(1)} %reduce_sum.9.st_ref) | copy-start | bytes 18436
  43.9 4.4 %collective-permute-start = (f32[12,128]{1,0:T(8,128)S(1)}, f32[12,128]{1,0:T(8,128)S(1)}, u32[]{:S(2)}, u32[]{:S(2)}) collective-permute-start(f32[12,128]{1,0:T(8,128)S(1)} %reduce_sum.9.st_ref), channel_id=1, source_target_pairs={{0,32},{32,0},{64,96},{96,64},{128,160},{160,128},{192,224},{224,1... | collective-permute-start | bytes 18440 | tf_op jit(solution)/shard_map/ppermute | solution.py:381
  48.4 0.6 copy-start.2
  63.7 28.5 %copy-start = (f32[2,4,2,16,768]{4,3,2,1,0:T(8,128)S(1)}, f32[2,4,2,16,768]{4,3,2,1,0:T(8,128)}, u32[]{:S(2)}) copy-start(f32[2,4,2,16,768]{4,3,2,1,0:T(8,128)} %get-tuple-element.24) | copy-start | bytes 2359300
  63.7 14.7 %collective-permute-start.2 = (f32[2,4,2,16,768]{4,3,2,1,0:T(8,128)}, f32[2,4,2,16,768]{4,3,2,1,0:T(8,128)S(1)}, u32[]{:S(2)}, u32[]{:S(2)}) collective-permute-start(f32[2,4,2,16,768]{4,3,2,1,0:T(8,128)} %get-tuple-element.23), channel_id=1, source_target_pairs={{0,1},{1,0},{2,3},{3,2},{4,5},{5,4},{6,7},{7,6},{8,9},{9,8},{10,11... | collective-permute-start | bytes 2359304 | tf_op jit(solution)/shard_map/ppermute | solution.py:378
  66.7 14.6 %collective-permute-start.4 = (f32[2,4,2,16,768]{4,3,2,1,0:T(8,128)}, f32[2,4,2,16,768]{4,3,2,1,0:T(8,128)S(1)}, u32[]{:S(2)}, u32[]{:S(2)}) collective-permute-start(f32[2,4,2,16,768]{4,3,2,1,0:T(8,128)} %get-tuple-element.25), channel_id=1, source_target_pairs={{0,4},{1,5},{2,6},{3,7},{4,0},{5,1},{6,2},{7,3},{8,12},{9,13},{10,... | collective-permute-start | bytes 2359304 | tf_op jit(solution)/shard_map/ppermute | solution.py:378
  79.4 10.1 %collective-permute-start.3 = (f32[4,2,16,768]{3,2,1,0:T(8,128)S(1)}, f32[4,2,16,768]{3,2,1,0:T(8,128)S(1)}, u32[]{:S(2)}, u32[]{:S(2)}) collective-permute-start(f32[4,2,16,768]{3,2,1,0:T(8,128)S(1)} %fusion.3), channel_id=1, source_target_pairs={{0,4},{1,5},{2,6},{3,7},{4,0},{5,1},{6,2},{7,3},{8,12},{9,13},{10,... | collective-permute-start | bytes 1179656 | tf_op jit(solution)/shard_map/ppermute | solution.py:378
  82.4 9.7 %collective-permute-start.5 = (f32[4,2,16,768]{3,2,1,0:T(8,128)S(1)}, f32[4,2,16,768]{3,2,1,0:T(8,128)S(1)}, u32[]{:S(2)}, u32[]{:S(2)}) collective-permute-start(f32[4,2,16,768]{3,2,1,0:T(8,128)S(1)} %fusion), channel_id=1, source_target_pairs={{0,1},{1,0},{2,3},{3,2},{4,5},{5,4},{6,7},{7,6},{8,9},{9,8},{10,11... | collective-permute-start | bytes 1179656 | tf_op jit(solution)/shard_map/ppermute | solution.py:378
  93.2 27.4 %all-to-all-start.1 = ((f32[8,16,1536]{2,1,0:T(8,128)}), f32[8,16,1536]{2,1,0:T(8,128)S(1)}, u32[]{:S(2)}, u32[]{:S(2)}) async-start(f32[8,16,1536]{2,1,0:T(8,128)} %bitcast.11), calls=%async_computation.1 | async-start | bytes 1572864 | tf_op jit(solution)/shard_map/all_to_all | solution.py:404
Sparse Core Ops, SparseCore 0:
  57.7 54.0 reduce-scatter.1

commit v4 on v3

--- a/solution.py
+++ b/solution.py
@@ -49,7 +49,7 @@
 
 
 SCORE_STEPS = 4
-SCORE_COPIES = 4 + 4 * SCORE_STEPS
+SCORE_COPIES = 3 + 4 * SCORE_STEPS
 
 
 def score_kernel(
@@ -62,7 +62,8 @@
     rows = m // SCORE_STEPS
     parts = [pl.ds(k * rows, rows) for k in range(SCORE_STEPS)]
     copies = Copies(sems)
-    a_copy = copies.start(a_hbm, a_ref)
+    a_parts = [pl.ds(r, LANES) for r in range(0, n, LANES)]
+    a_copies = [copies.start(a_hbm.at[part], a_ref.at[part]) for part in a_parts]
     c_copies = [copies.start(c_hbm.at[part], c_ref.at[part]) for part in parts]
     out = []
     for k in range(0, m, LANES):
@@ -74,8 +75,8 @@
     x_ref[m + n : m + n + SPARE, :] = jnp.zeros((SPARE, n), F32)
     x_ref[m + n : m + n + 1, :] = ag
     x_ref[m + n + 1 : m + n + 2, :] = cot_ref[...]
-    a_copy.wait()
-    for r in range(0, n, LANES):
+    for r, a_copy in zip(range(0, n, LANES), a_copies):
+        a_copy.wait()
         values = a_ref[r : r + LANES, :].astype(F32)
         unit = values * inverse_radius(values)
         full_ref[r : r + LANES, :] = unit.astype(BF16)
@@ -144,7 +145,7 @@
             pltpu.VMEM((n, width), BF16),
             *(pltpu.VMEM(*s) for s in shapes),
             pltpu.VMEM((SLOTS, LANES), F32),
-            pltpu.SemaphoreType.DMA((SCORE_COPIES,)),
+            pltpu.SemaphoreType.DMA((SCORE_COPIES + n // LANES,)),
         ],
         compiler_params=pltpu.CompilerParams(vmem_limit_bytes=62 * MIB),
         name="scores",
@@ -152,7 +153,7 @@
 
 
 CANDIDATE_STEPS = 3
-CANDIDATE_COPIES = 3 + 6 * CANDIDATE_STEPS
+CANDIDATE_COPIES = 4 + 6 * CANDIDATE_STEPS
 
 
 def candidate_kernel(
@@ -168,19 +169,19 @@
     wide = more_ref.shape[1]
     parts = [pl.ds(k * rows, rows) for k in range(CANDIDATE_STEPS)]
     copies = Copies(sems)
-    extra_copy = copies.start(y_hbm.at[pl.ds(m, n + SPARE)], extra_ref)
-    more_copy = copies.start(
-        y_hbm.at[pl.ds(m + n + SPARE, n), pl.ds(0, wide)], more_ref
-    )
-    an_copy = copies.start(an_hbm, an_ref.at[pl.ds(0, n)])
-    ready = []
-    for part in parts:
+    spare_copy = copies.start(y_hbm.at[pl.ds(m + n, SPARE)], extra_ref.at[pl.ds(n, SPARE)])
+    ready, late = [], []
+    for k, part in enumerate(parts):
         ready.append([copies.start(row_hbm.at[:, part], row_ref.at[:, part])])
         for side in range(2):
             place = pl.ds(side * half + part.start, rows)
-            ready[-1].append(copies.start(x_hbm.at[place], x_ref.at[side, part]))
-            ready[-1].append(copies.start(y_hbm.at[place], y_ref.at[side, part]))
-        ready[-1].append(copies.start(cc_hbm.at[:, part], cc_ref.at[:, part]))
+            ready[k].append(copies.start(x_hbm.at[place], x_ref.at[side, part]))
+            ready[k].append(copies.start(y_hbm.at[place], y_ref.at[side, part]))
+        if k == 0:
+            an_copy = copies.start(an_hbm, an_ref.at[pl.ds(0, n)])
+            extra_copy = copies.start(y_hbm.at[pl.ds(m, n)], extra_ref.at[pl.ds(0, n)])
+            more_copy = copies.start(y_hbm.at[pl.ds(m + n + SPARE, n), pl.ds(0, wide)], more_ref)
+        late.append(copies.start(cc_hbm.at[:, part], cc_ref.at[:, part]))
     out = []
 
     def sums(ref):
@@ -193,13 +194,10 @@
 
     total, count, positive = sums(st_ref)
     cost_ref[...] = SCALE + jnp.log(total) - positive / count
-    extra_copy.wait()
+    spare_copy.wait()
     factors = [(SCALE * cot_ref[...], 1.0 / total, 1.0 / count, ag_ref[...].astype(F32))]
     total, count, _ = sums(other_ref)
     factors.append((SCALE * extra_ref[n + 1 : n + 2, :], 1.0 / total, 1.0 / count, extra_ref[n : n + 1, :]))
-    an_ref[n:, :n] = extra_ref[:n, :].astype(BF16)
-    more_copy.wait()
-    an_ref[n:, n:] = more_ref[...].astype(BF16)
     low = lax.broadcasted_iota(jnp.int32, (rows, LANES), 1) < LANES // 2
 
     def coefficients(ref, side, part, factor):
@@ -221,7 +219,12 @@
             coefs.append((jnp.concatenate([mine, theirs], axis=1), inner + more))
         out.append(copies.start(coef_ref.at[:, part], coef_hbm.at[:, part]))
         if k == 0:
+            extra_copy.wait()
+            an_ref[n:, :n] = extra_ref[:n, :].astype(BF16)
+            more_copy.wait()
+            an_ref[n:, n:] = more_ref[...].astype(BF16)
             an_copy.wait()
+        late[k].wait()
         grads = []
         for side, (coef, inner) in enumerate(coefs):
             dcn = jnp.dot(coef, an_ref[...], preferred_element_type=F32)

time: 131 us -> 131 us (level)
  no operation moved by 1% of the time
where the time goes in v4:
time: 131 us; the launch traced here: 130 us
  waiting for transfers between devices  37.7 us (29%)
  starting transfers between devices  31 us (24%)
  Pallas kernels  25.4 us (19%)
  blocking collectives  16 us (12%)
  between operations  14.1 us (11%)
  other arithmetic  4.25 us (3%)
  local copies, waits for them, and re-layouts  1.4 us (1%)
    all_to_all x1, waiting for transfers between devices, per_device(): lax.all_to_all(terms, 'cand', 0, 0, axis_index_groups=groups, tiled=True)  21.8 us
    ppermute x2, starting transfers between devices, sibling(): return lax.ppermute(v, 'anc', [(p, p ^ 1) for p in range(n_anc)])  16.2 us
    all_to_all x1, blocking collectives, per_device(): st = jnp.sum(lax.all_to_all(st, 'cand', 0, 0, tiled=True), axis=0)  16 us
    ppermute x4, waiting for transfers between devices, swap(): return lax.ppermute(v, ('anc', 'cand'), pairs)  15.3 us
    ppermute x4, starting transfers between devices, swap(): return lax.ppermute(v, ('anc', 'cand'), pairs)  9.99 us
    pallas_call x1, Pallas kernels, candidate_stage(): pl.pallas_call(candidate_kernel, in_specs=[VMEM] * 4 + [HBM] * 5, out_spe...  8.57 us
    pallas_call x1, Pallas kernels, score_stage(): pl.pallas_call(score_kernel, in_specs=[HBM, HBM, VMEM, VMEM, VMEM], out_s...  8.04 us
    pallas_call x1, Pallas kernels, anchor_stage(): pl.pallas_call(anchor_kernel, in_specs=[HBM, HBM, HBM], out_specs=[HBM] *...  6.08 us
  transfers between devices with their start and end apart: 8, of which 5 were waited for; matrix products, arithmetic and copies ran while one was open for 4% of the time, Pallas kernels for 5%

profile of v4, /device:TPU:1, one launch (start us, length us, event | category | flops | bytes accessed | tf_op | source)
XLA Modules:
  0.0 129.9 jit_solution(14864157271766905122)
XLA Ops:
  7.2 8.0 %scores.1 = (bf16[512,768]{1,0:T(8,128)(2,1)}, f32[1992,512]{1,0:T(8,128)}, f32[32,12,128]{2,1,0:T(8,128)}, f32[960,128]{1,0:T(8,128)}, bf16[960,768]{1,0:T(8,128)(2,1)}) custom-call(bf16[512,1536]{1,0:T(8,128)(2,1)} %a_hbm.1, bf16[960,1536]{1,0:T(8,128)(2,1)} %c_hbm.3, s32[1,512]{1,0:T(1,128)} %bitcast.26, s32[1,960]{1,0:T(1,128)} %bitcast.30, ...), custom_call_target="tpu_custom_call" | custom-call | tf_op jit(solution)/shard_map/scores/pallas_call | solution.py:137
  15.3 12.4 %collective-permute-start.1 = (f32[1992,512]{1,0:T(8,128)}, f32[1992,512]{1,0:T(8,128)}, u32[]{:S(2)}, u32[]{:S(2)}) collective-permute-start(f32[1992,512]{1,0:T(8,128)} %get-tuple-element.19.x_hbm), channel_id=1, source_target_pairs={{0,32},{32,0},{64,96},{96,64},{128,160},{160,128},{192,224},{224,1... | collective-permute-start | bytes 12238856 | tf_op jit(solution)/shard_map/ppermute | solution.py:384
  27.7 16.0 %all_to_all.10 = f32[32,12,128]{2,1,0:T(8,128)S(1)} all-to-all(f32[32,12,128]{2,1,0:T(8,128)} %get-tuple-element.15), channel_id=1, replica_groups=mesh['anc'=24,'cand'=32] {'cand'}, dimensions={0} | all-to-all | bytes 393216 | tf_op jit(solution)/shard_map/all_to_all | solution.py:390
  43.8 3.8 %collective-permute-start = (f32[12,128]{1,0:T(8,128)S(1)}, f32[12,128]{1,0:T(8,128)S(1)}, u32[]{:S(2)}, u32[]{:S(2)}) collective-permute-start(f32[12,128]{1,0:T(8,128)S(1)} %reduce_sum.9.st_ref), channel_id=1, source_target_pairs={{0,32},{32,0},{64,96},{96,64},{128,160},{160,128},{192,224},{224,1... | collective-permute-start | bytes 18440 | tf_op jit(solution)/shard_map/ppermute | solution.py:384
  47.6 0.6 collective-permute-done.other_ref
  48.2 0.6 copy-done.2
  48.8 8.6 %candidate_terms.1 = (f32[1,512]{1,0:T(1,128)}, bf16[2,480,512]{2,1,0:T(8,128)(2,1)}, f32[12,480,128]{2,1,0:T(8,128)}) custom-call(f32[12,128]{1,0:T(8,128)} %copy-done.1, f32[12,128]{1,0:T(8,128)} %copy-done.2, f32[1,512]{1,0:T(1,128)} %bitcast.29, s32[1,512]{1,0:T(1,128)} %bitcast.27, f32[2,480,128]{2,1,0:T(8,128)} %bitcast.23, ...), custom_call_target="tpu_custom_call" | custom-call | tf_op jit(solution)/shard_map/candidate_terms/pallas_call | solution.py:258
  57.4 6.1 %anchor_terms.1 = (f32[2,4,2,16,768]{4,3,2,1,0:T(8,128)}, f32[2,4,2,16,768]{4,3,2,1,0:T(8,128)}, f32[2,4,2,16,768]{4,3,2,1,0:T(8,128)}, f32[2,4,2,16,768]{4,3,2,1,0:T(8,128)}) custom-call(bf16[960,512]{1,0:T(8,128)(2,1)} %bitcast.31, f32[960,128]{1,0:T(8,128)} %get-tuple-element.16.row_hbm, bf16[960,1536]{1,0:T(8,128)(2,1)} %c_hbm.3), custom_call_target="tpu_custom_call" | custom-call | flops 1509949440 | bytes 8388608 | tf_op jit(solution)/shard_map/anchor_terms/pallas_call | solution.py:312
  63.5 3.0 %collective-permute-start.2 = (f32[2,4,2,16,768]{4,3,2,1,0:T(8,128)}, f32[2,4,2,16,768]{4,3,2,1,0:T(8,128)S(1)}, u32[]{:S(2)}, u32[]{:S(2)}) collective-permute-start(f32[2,4,2,16,768]{4,3,2,1,0:T(8,128)} %get-tuple-element.23), channel_id=1, source_target_pairs={{0,1},{1,0},{2,3},{3,2},{4,5},{5,4},{6,7},{7,6},{8,9},{9,8},{10,11... | collective-permute-start | bytes 2359304 | tf_op jit(solution)/shard_map/ppermute | solution.py:381
  66.5 1.9 %collective-permute-start.4 = (f32[2,4,2,16,768]{4,3,2,1,0:T(8,128)}, f32[2,4,2,16,768]{4,3,2,1,0:T(8,128)S(1)}, u32[]{:S(2)}, u32[]{:S(2)}) collective-permute-start(f32[2,4,2,16,768]{4,3,2,1,0:T(8,128)} %get-tuple-element.25), channel_id=1, source_target_pairs={{0,4},{1,5},{2,6},{3,7},{4,0},{5,1},{6,2},{7,3},{8,12},{9,13},{10,... | collective-permute-start | bytes 2359304 | tf_op jit(solution)/shard_map/ppermute | solution.py:381
  68.5 9.7 %collective-permute-done.2 = f32[2,4,2,16,768]{4,3,2,1,0:T(8,128)S(1)} collective-permute-done((f32[2,4,2,16,768]{4,3,2,1,0:T(8,128)}, f32[2,4,2,16,768]{4,3,2,1,0:T(8,128)S(1)}, u32[]{:S(2)}, u32[]{:S(2)}) %collective-permute-start.2) | collective-permute-done | bytes 786464 | tf_op jit(solution)/shard_map/ppermute | solution.py:381
  78.2 1.0 fusion.3
  79.2 1.9 %collective-permute-start.3 = (f32[4,2,16,768]{3,2,1,0:T(8,128)S(1)}, f32[4,2,16,768]{3,2,1,0:T(8,128)S(1)}, u32[]{:S(2)}, u32[]{:S(2)}) collective-permute-start(f32[4,2,16,768]{3,2,1,0:T(8,128)S(1)} %fusion.3), channel_id=1, source_target_pairs={{0,4},{1,5},{2,6},{3,7},{4,0},{5,1},{6,2},{7,3},{8,12},{9,13},{10,... | collective-permute-start | bytes 1179656 | tf_op jit(solution)/shard_map/ppermute | solution.py:381
  81.2 1.1 fusion
  82.2 3.1 %collective-permute-start.5 = (f32[4,2,16,768]{3,2,1,0:T(8,128)S(1)}, f32[4,2,16,768]{3,2,1,0:T(8,128)S(1)}, u32[]{:S(2)}, u32[]{:S(2)}) collective-permute-start(f32[4,2,16,768]{3,2,1,0:T(8,128)S(1)} %fusion), channel_id=1, source_target_pairs={{0,1},{1,0},{2,3},{3,2},{4,5},{5,4},{6,7},{7,6},{8,9},{9,8},{10,11... | collective-permute-start | bytes 1179656 | tf_op jit(solution)/shard_map/ppermute | solution.py:381
  85.4 4.0 %collective-permute-done.3 = f32[4,2,16,768]{3,2,1,0:T(8,128)S(1)} collective-permute-done((f32[4,2,16,768]{3,2,1,0:T(8,128)S(1)}, f32[4,2,16,768]{3,2,1,0:T(8,128)S(1)}, u32[]{:S(2)}, u32[]{:S(2)}) %collective-permute-start.3) | collective-permute-done | bytes 393248 | tf_op jit(solution)/shard_map/ppermute | solution.py:381
  89.4 1.1 fusion.5
  90.4 1.5 %collective-permute-done.5 = f32[4,2,16,768]{3,2,1,0:T(8,128)S(1)} collective-permute-done((f32[4,2,16,768]{3,2,1,0:T(8,128)S(1)}, f32[4,2,16,768]{3,2,1,0:T(8,128)S(1)}, u32[]{:S(2)}, u32[]{:S(2)}) %collective-permute-start.5) | collective-permute-done | bytes 393248 | tf_op jit(solution)/shard_map/ppermute | solution.py:381
  92.1 1.0 pad_maximum_fusion
  93.0 4.7 %all-to-all-start.1 = ((f32[8,16,1536]{2,1,0:T(8,128)}), f32[8,16,1536]{2,1,0:T(8,128)S(1)}, u32[]{:S(2)}, u32[]{:S(2)}) async-start(f32[8,16,1536]{2,1,0:T(8,128)} %bitcast.11), calls=%async_computation.1 | async-start | bytes 1572864 | tf_op jit(solution)/shard_map/all_to_all | solution.py:407
  97.7 0.8 constant_dynamic-slice_fusion.a_ref
  98.5 21.8 %all-to-all-done.1.t_ref = f32[8,16,1536]{2,1,0:T(8,128)S(1)} async-done(((f32[8,16,1536]{2,1,0:T(8,128)}), f32[8,16,1536]{2,1,0:T(8,128)S(1)}, u32[]{:S(2)}, u32[]{:S(2)}) %all-to-all-start.1) | async-done | bytes 786464 | tf_op jit(solution)/shard_map/all_to_all | solution.py:407
  120.3 0.8 probe_derivatives.1
  121.2 1.9 %unpack.1 = f32[64,960]{1,0:T(8,128)} custom-call(f32[480,128]{1,0:T(8,128)} %bitcast.25), custom_call_target="tpu_custom_call" | custom-call | tf_op jit(solution)/shard_map/unpack/pallas_call | solution.py:358
  (12 shorter events, 0.2 us)
Async XLA Ops:
  7.2 114.0 %reduce-scatter.2.cloned.1.call-start = ((), (), s32[]{:S(2)}) async-start(), calls=%async_computation.3 | async-start | bytes 3194880 | tf_op jit(solution)/shard_map/reduce_scatter | solution.py:392
  15.3 32.9 %collective-permute-start.1 = (f32[1992,512]{1,0:T(8,128)}, f32[1992,512]{1,0:T(8,128)}, u32[]{:S(2)}, u32[]{:S(2)}) collective-permute-start(f32[1992,512]{1,0:T(8,128)} %get-tuple-element.19.x_hbm), channel_id=1, source_target_pairs={{0,32},{32,0},{64,96},{96,64},{128,160},{160,128},{192,224},{224,1... | collective-permute-start | bytes 12238856 | tf_op jit(solution)/shard_map/ppermute | solution.py:384
  43.7 4.5 %copy-start.1 = (f32[12,128]{1,0:T(8,128)}, f32[12,128]{1,0:T(8,128)S(1)}, u32[]{:S(2)}) copy-start(f32[12,128]{1,0:T(8,128)S(1)} %reduce_sum.9.st_ref) | copy-start | bytes 18436
  43.8 4.4 %collective-permute-start = (f32[12,128]{1,0:T(8,128)S(1)}, f32[12,128]{1,0:T(8,128)S(1)}, u32[]{:S(2)}, u32[]{:S(2)}) collective-permute-start(f32[12,128]{1,0:T(8,128)S(1)} %reduce_sum.9.st_ref), channel_id=1, source_target_pairs={{0,32},{32,0},{64,96},{96,64},{128,160},{160,128},{192,224},{224,1... | collective-permute-start | bytes 18440 | tf_op jit(solution)/shard_map/ppermute | solution.py:384
  48.2 0.6 copy-start.2
  63.5 28.5 %copy-start = (f32[2,4,2,16,768]{4,3,2,1,0:T(8,128)S(1)}, f32[2,4,2,16,768]{4,3,2,1,0:T(8,128)}, u32[]{:S(2)}) copy-start(f32[2,4,2,16,768]{4,3,2,1,0:T(8,128)} %get-tuple-element.24) | copy-start | bytes 2359300
  63.5 14.7 %collective-permute-start.2 = (f32[2,4,2,16,768]{4,3,2,1,0:T(8,128)}, f32[2,4,2,16,768]{4,3,2,1,0:T(8,128)S(1)}, u32[]{:S(2)}, u32[]{:S(2)}) collective-permute-start(f32[2,4,2,16,768]{4,3,2,1,0:T(8,128)} %get-tuple-element.23), channel_id=1, source_target_pairs={{0,1},{1,0},{2,3},{3,2},{4,5},{5,4},{6,7},{7,6},{8,9},{9,8},{10,11... | collective-permute-start | bytes 2359304 | tf_op jit(solution)/shard_map/ppermute | solution.py:381
  66.5 14.6 %collective-permute-start.4 = (f32[2,4,2,16,768]{4,3,2,1,0:T(8,128)}, f32[2,4,2,16,768]{4,3,2,1,0:T(8,128)S(1)}, u32[]{:S(2)}, u32[]{:S(2)}) collective-permute-start(f32[2,4,2,16,768]{4,3,2,1,0:T(8,128)} %get-tuple-element.25), channel_id=1, source_target_pairs={{0,4},{1,5},{2,6},{3,7},{4,0},{5,1},{6,2},{7,3},{8,12},{9,13},{10,... | collective-permute-start | bytes 2359304 | tf_op jit(solution)/shard_map/ppermute | solution.py:381
  79.2 10.1 %collective-permute-start.3 = (f32[4,2,16,768]{3,2,1,0:T(8,128)S(1)}, f32[4,2,16,768]{3,2,1,0:T(8,128)S(1)}, u32[]{:S(2)}, u32[]{:S(2)}) collective-permute-start(f32[4,2,16,768]{3,2,1,0:T(8,128)S(1)} %fusion.3), channel_id=1, source_target_pairs={{0,4},{1,5},{2,6},{3,7},{4,0},{5,1},{6,2},{7,3},{8,12},{9,13},{10,... | collective-permute-start | bytes 1179656 | tf_op jit(solution)/shard_map/ppermute | solution.py:381
  82.2 9.7 %collective-permute-start.5 = (f32[4,2,16,768]{3,2,1,0:T(8,128)S(1)}, f32[4,2,16,768]{3,2,1,0:T(8,128)S(1)}, u32[]{:S(2)}, u32[]{:S(2)}) collective-permute-start(f32[4,2,16,768]{3,2,1,0:T(8,128)S(1)} %fusion), channel_id=1, source_target_pairs={{0,1},{1,0},{2,3},{3,2},{4,5},{5,4},{6,7},{7,6},{8,9},{9,8},{10,11... | collective-permute-start | bytes 1179656 | tf_op jit(solution)/shard_map/ppermute | solution.py:381
  93.0 27.3 %all-to-all-start.1 = ((f32[8,16,1536]{2,1,0:T(8,128)}), f32[8,16,1536]{2,1,0:T(8,128)S(1)}, u32[]{:S(2)}, u32[]{:S(2)}) async-start(f32[8,16,1536]{2,1,0:T(8,128)} %bitcast.11), calls=%async_computation.1 | async-start | bytes 1572864 | tf_op jit(solution)/shard_map/all_to_all | solution.py:407
Sparse Core Ops, SparseCore 0:
  57.5 54.0 reduce-scatter.1

commit v5 on v4

--- a/solution.py
+++ b/solution.py
@@ -48,7 +48,7 @@
     return blocks
 
 
-SCORE_STEPS = 4
+SCORE_STEPS = 3
 SCORE_COPIES = 3 + 4 * SCORE_STEPS
 
 
@@ -225,11 +225,15 @@
             an_ref[n:, n:] = more_ref[...].astype(BF16)
             an_copy.wait()
         late[k].wait()
+        dcn = jnp.dot(
+            jnp.concatenate([coef for coef, _ in coefs], axis=0), an_ref[...],
+            preferred_element_type=F32,
+        )
         grads = []
-        for side, (coef, inner) in enumerate(coefs):
-            dcn = jnp.dot(coef, an_ref[...], preferred_element_type=F32)
+        for side, (_, inner) in enumerate(coefs):
             inv = row_ref[side, part, :1]
-            grads.append(inv * (dcn - cc_ref[side, part, :].astype(F32) * (inv * inner)))
+            term = dcn[side * rows : (side + 1) * rows]
+            grads.append(inv * (term - cc_ref[side, part, :].astype(F32) * (inv * inner)))
         over, under = grads
         for b in range(own_ref.shape[0] // 2):
             top = over[:, b * LANES : (b + 1) * LANES]

time: 131 us -> 131 us (level)
  no operation moved by 1% of the time
where the time goes in v5:
time: 131 us; the launch traced here: 130 us
  waiting for transfers between devices  37.7 us (29%)
  starting transfers between devices  31 us (24%)
  Pallas kernels  25.4 us (19%)
  blocking collectives  16 us (12%)
  between operations  14.1 us (11%)
  other arithmetic  4.25 us (3%)
  local copies, waits for them, and re-layouts  1.4 us (1%)
    all_to_all x1, waiting for transfers between devices, per_device(): lax.all_to_all(terms, 'cand', 0, 0, axis_index_groups=groups, tiled=True)  21.8 us
    ppermute x2, starting transfers between devices, sibling(): return lax.ppermute(v, 'anc', [(p, p ^ 1) for p in range(n_anc)])  16.3 us
    all_to_all x1, blocking collectives, per_device(): st = jnp.sum(lax.all_to_all(st, 'cand', 0, 0, tiled=True), axis=0)  16 us
    ppermute x4, waiting for transfers between devices, swap(): return lax.ppermute(v, ('anc', 'cand'), pairs)  15.3 us
    ppermute x4, starting transfers between devices, swap(): return lax.ppermute(v, ('anc', 'cand'), pairs)  9.99 us
    pallas_call x1, Pallas kernels, candidate_stage(): pl.pallas_call(candidate_kernel, in_specs=[VMEM] * 4 + [HBM] * 5, out_spe...  8.83 us
    pallas_call x1, Pallas kernels, score_stage(): pl.pallas_call(score_kernel, in_specs=[HBM, HBM, VMEM, VMEM, VMEM], out_s...  7.8 us
    pallas_call x1, Pallas kernels, anchor_stage(): pl.pallas_call(anchor_kernel, in_specs=[HBM, HBM, HBM], out_specs=[HBM] *...  6.08 us
  transfers between devices with their start and end apart: 8, of which 5 were waited for; matrix products, arithmetic and copies ran while one was open for 4% of the time, Pallas kernels for 5%

profile of v5, /device:TPU:1, one launch (start us, length us, event | category | flops | bytes accessed | tf_op | source)
XLA Modules:
  0.0 130.0 jit_solution(17910134246286299744)
XLA Ops:
  7.2 7.8 %scores.1 = (bf16[512,768]{1,0:T(8,128)(2,1)}, f32[1992,512]{1,0:T(8,128)}, f32[32,12,128]{2,1,0:T(8,128)}, f32[960,128]{1,0:T(8,128)}, bf16[960,768]{1,0:T(8,128)(2,1)}) custom-call(bf16[512,1536]{1,0:T(8,128)(2,1)} %a_hbm.1, bf16[960,1536]{1,0:T(8,128)(2,1)} %c_hbm.3, s32[1,512]{1,0:T(1,128)} %bitcast.26, s32[1,960]{1,0:T(1,128)} %bitcast.30, ...), custom_call_target="tpu_custom_call" | custom-call | tf_op jit(solution)/shard_map/scores/pallas_call | solution.py:137
  15.0 12.5 %collective-permute-start.1 = (f32[1992,512]{1,0:T(8,128)}, f32[1992,512]{1,0:T(8,128)}, u32[]{:S(2)}, u32[]{:S(2)}) collective-permute-start(f32[1992,512]{1,0:T(8,128)} %get-tuple-element.19.x_hbm), channel_id=1, source_target_pairs={{0,32},{32,0},{64,96},{96,64},{128,160},{160,128},{192,224},{224,1... | collective-permute-start | bytes 12238856 | tf_op jit(solution)/shard_map/ppermute | solution.py:388
  27.5 16.0 %all_to_all.10 = f32[32,12,128]{2,1,0:T(8,128)S(1)} all-to-all(f32[32,12,128]{2,1,0:T(8,128)} %get-tuple-element.15), channel_id=1, replica_groups=mesh['anc'=24,'cand'=32] {'cand'}, dimensions={0} | all-to-all | bytes 393216 | tf_op jit(solution)/shard_map/all_to_all | solution.py:394
  43.6 3.8 %collective-permute-start = (f32[12,128]{1,0:T(8,128)S(1)}, f32[12,128]{1,0:T(8,128)S(1)}, u32[]{:S(2)}, u32[]{:S(2)}) collective-permute-start(f32[12,128]{1,0:T(8,128)S(1)} %reduce_sum.9.st_ref), channel_id=1, source_target_pairs={{0,32},{32,0},{64,96},{96,64},{128,160},{160,128},{192,224},{224,1... | collective-permute-start | bytes 18440 | tf_op jit(solution)/shard_map/ppermute | solution.py:388
  47.4 0.6 collective-permute-done.other_ref
  48.0 0.6 copy-done.2
  48.6 8.8 %candidate_terms.1 = (f32[1,512]{1,0:T(1,128)}, bf16[2,480,512]{2,1,0:T(8,128)(2,1)}, f32[12,480,128]{2,1,0:T(8,128)}) custom-call(f32[12,128]{1,0:T(8,128)} %copy-done.1, f32[12,128]{1,0:T(8,128)} %copy-done.2, f32[1,512]{1,0:T(1,128)} %bitcast.29, s32[1,512]{1,0:T(1,128)} %bitcast.27, f32[2,480,128]{2,1,0:T(8,128)} %bitcast.23, ...), custom_call_target="tpu_custom_call" | custom-call | tf_op jit(solution)/shard_map/candidate_terms/pallas_call | solution.py:262
  57.5 6.1 %anchor_terms.1 = (f32[2,4,2,16,768]{4,3,2,1,0:T(8,128)}, f32[2,4,2,16,768]{4,3,2,1,0:T(8,128)}, f32[2,4,2,16,768]{4,3,2,1,0:T(8,128)}, f32[2,4,2,16,768]{4,3,2,1,0:T(8,128)}) custom-call(bf16[960,512]{1,0:T(8,128)(2,1)} %bitcast.31, f32[960,128]{1,0:T(8,128)} %get-tuple-element.16.row_hbm, bf16[960,1536]{1,0:T(8,128)(2,1)} %c_hbm.3), custom_call_target="tpu_custom_call" | custom-call | flops 1509949440 | bytes 8388608 | tf_op jit(solution)/shard_map/anchor_terms/pallas_call | solution.py:316
  63.6 3.0 %collective-permute-start.2 = (f32[2,4,2,16,768]{4,3,2,1,0:T(8,128)}, f32[2,4,2,16,768]{4,3,2,1,0:T(8,128)S(1)}, u32[]{:S(2)}, u32[]{:S(2)}) collective-permute-start(f32[2,4,2,16,768]{4,3,2,1,0:T(8,128)} %get-tuple-element.23), channel_id=1, source_target_pairs={{0,1},{1,0},{2,3},{3,2},{4,5},{5,4},{6,7},{7,6},{8,9},{9,8},{10,11... | collective-permute-start | bytes 2359304 | tf_op jit(solution)/shard_map/ppermute | solution.py:385
  66.6 1.9 %collective-permute-start.4 = (f32[2,4,2,16,768]{4,3,2,1,0:T(8,128)}, f32[2,4,2,16,768]{4,3,2,1,0:T(8,128)S(1)}, u32[]{:S(2)}, u32[]{:S(2)}) collective-permute-start(f32[2,4,2,16,768]{4,3,2,1,0:T(8,128)} %get-tuple-element.25), channel_id=1, source_target_pairs={{0,4},{1,5},{2,6},{3,7},{4,0},{5,1},{6,2},{7,3},{8,12},{9,13},{10,... | collective-permute-start | bytes 2359304 | tf_op jit(solution)/shard_map/ppermute | solution.py:385
  68.6 9.7 %collective-permute-done.2 = f32[2,4,2,16,768]{4,3,2,1,0:T(8,128)S(1)} collective-permute-done((f32[2,4,2,16,768]{4,3,2,1,0:T(8,128)}, f32[2,4,2,16,768]{4,3,2,1,0:T(8,128)S(1)}, u32[]{:S(2)}, u32[]{:S(2)}) %collective-permute-start.2) | collective-permute-done | bytes 786464 | tf_op jit(solution)/shard_map/ppermute | solution.py:385
  78.3 1.0 fusion.3
  79.3 1.9 %collective-permute-start.3 = (f32[4,2,16,768]{3,2,1,0:T(8,128)S(1)}, f32[4,2,16,768]{3,2,1,0:T(8,128)S(1)}, u32[]{:S(2)}, u32[]{:S(2)}) collective-permute-start(f32[4,2,16,768]{3,2,1,0:T(8,128)S(1)} %fusion.3), channel_id=1, source_target_pairs={{0,4},{1,5},{2,6},{3,7},{4,0},{5,1},{6,2},{7,3},{8,12},{9,13},{10,... | collective-permute-start | bytes 1179656 | tf_op jit(solution)/shard_map/ppermute | solution.py:385
  81.3 1.1 fusion
  82.3 3.1 %collective-permute-start.5 = (f32[4,2,16,768]{3,2,1,0:T(8,128)S(1)}, f32[4,2,16,768]{3,2,1,0:T(8,128)S(1)}, u32[]{:S(2)}, u32[]{:S(2)}) collective-permute-start(f32[4,2,16,768]{3,2,1,0:T(8,128)S(1)} %fusion), channel_id=1, source_target_pairs={{0,1},{1,0},{2,3},{3,2},{4,5},{5,4},{6,7},{7,6},{8,9},{9,8},{10,11... | collective-permute-start | bytes 1179656 | tf_op jit(solution)/shard_map/ppermute | solution.py:385
  85.4 4.0 %collective-permute-done.3 = f32[4,2,16,768]{3,2,1,0:T(8,128)S(1)} collective-permute-done((f32[4,2,16,768]{3,2,1,0:T(8,128)S(1)}, f32[4,2,16,768]{3,2,1,0:T(8,128)S(1)}, u32[]{:S(2)}, u32[]{:S(2)}) %collective-permute-start.3) | collective-permute-done | bytes 393248 | tf_op jit(solution)/shard_map/ppermute | solution.py:385
  89.4 1.1 fusion.5
  90.5 1.5 %collective-permute-done.5 = f32[4,2,16,768]{3,2,1,0:T(8,128)S(1)} collective-permute-done((f32[4,2,16,768]{3,2,1,0:T(8,128)S(1)}, f32[4,2,16,768]{3,2,1,0:T(8,128)S(1)}, u32[]{:S(2)}, u32[]{:S(2)}) %collective-permute-start.5) | collective-permute-done | bytes 393248 | tf_op jit(solution)/shard_map/ppermute | solution.py:385
  92.1 1.0 pad_maximum_fusion
  93.1 4.7 %all-to-all-start.1 = ((f32[8,16,1536]{2,1,0:T(8,128)}), f32[8,16,1536]{2,1,0:T(8,128)S(1)}, u32[]{:S(2)}, u32[]{:S(2)}) async-start(f32[8,16,1536]{2,1,0:T(8,128)} %bitcast.11), calls=%async_computation.1 | async-start | bytes 1572864 | tf_op jit(solution)/shard_map/all_to_all | solution.py:411
  97.8 0.8 constant_dynamic-slice_fusion.a_ref
  98.6 21.8 %all-to-all-done.1.t_ref = f32[8,16,1536]{2,1,0:T(8,128)S(1)} async-done(((f32[8,16,1536]{2,1,0:T(8,128)}), f32[8,16,1536]{2,1,0:T(8,128)S(1)}, u32[]{:S(2)}, u32[]{:S(2)}) %all-to-all-start.1) | async-done | bytes 786464 | tf_op jit(solution)/shard_map/all_to_all | solution.py:411
  120.4 0.8 probe_derivatives.1
  121.3 1.9 %unpack.1 = f32[64,960]{1,0:T(8,128)} custom-call(f32[480,128]{1,0:T(8,128)} %bitcast.25), custom_call_target="tpu_custom_call" | custom-call | tf_op jit(solution)/shard_map/unpack/pallas_call | solution.py:362
  (12 shorter events, 0.2 us)
Async XLA Ops:
  7.2 114.1 %reduce-scatter.2.cloned.1.call-start = ((), (), s32[]{:S(2)}) async-start(), calls=%async_computation.3 | async-start | bytes 3194880 | tf_op jit(solution)/shard_map/reduce_scatter | solution.py:396
  15.0 33.0 %collective-permute-start.1 = (f32[1992,512]{1,0:T(8,128)}, f32[1992,512]{1,0:T(8,128)}, u32[]{:S(2)}, u32[]{:S(2)}) collective-permute-start(f32[1992,512]{1,0:T(8,128)} %get-tuple-element.19.x_hbm), channel_id=1, source_target_pairs={{0,32},{32,0},{64,96},{96,64},{128,160},{160,128},{192,224},{224,1... | collective-permute-start | bytes 12238856 | tf_op jit(solution)/shard_map/ppermute | solution.py:388
  43.6 4.5 %copy-start.1 = (f32[12,128]{1,0:T(8,128)}, f32[12,128]{1,0:T(8,128)S(1)}, u32[]{:S(2)}) copy-start(f32[12,128]{1,0:T(8,128)S(1)} %reduce_sum.9.st_ref) | copy-start | bytes 18436
  43.6 4.4 %collective-permute-start = (f32[12,128]{1,0:T(8,128)S(1)}, f32[12,128]{1,0:T(8,128)S(1)}, u32[]{:S(2)}, u32[]{:S(2)}) collective-permute-start(f32[12,128]{1,0:T(8,128)S(1)} %reduce_sum.9.st_ref), channel_id=1, source_target_pairs={{0,32},{32,0},{64,96},{96,64},{128,160},{160,128},{192,224},{224,1... | collective-permute-start | bytes 18440 | tf_op jit(solution)/shard_map/ppermute | solution.py:388
  48.0 0.6 copy-start.2
  63.6 28.5 %copy-start = (f32[2,4,2,16,768]{4,3,2,1,0:T(8,128)S(1)}, f32[2,4,2,16,768]{4,3,2,1,0:T(8,128)}, u32[]{:S(2)}) copy-start(f32[2,4,2,16,768]{4,3,2,1,0:T(8,128)} %get-tuple-element.24) | copy-start | bytes 2359300
  63.6 14.7 %collective-permute-start.2 = (f32[2,4,2,16,768]{4,3,2,1,0:T(8,128)}, f32[2,4,2,16,768]{4,3,2,1,0:T(8,128)S(1)}, u32[]{:S(2)}, u32[]{:S(2)}) collective-permute-start(f32[2,4,2,16,768]{4,3,2,1,0:T(8,128)} %get-tuple-element.23), channel_id=1, source_target_pairs={{0,1},{1,0},{2,3},{3,2},{4,5},{5,4},{6,7},{7,6},{8,9},{9,8},{10,11... | collective-permute-start | bytes 2359304 | tf_op jit(solution)/shard_map/ppermute | solution.py:385
  66.6 14.6 %collective-permute-start.4 = (f32[2,4,2,16,768]{4,3,2,1,0:T(8,128)}, f32[2,4,2,16,768]{4,3,2,1,0:T(8,128)S(1)}, u32[]{:S(2)}, u32[]{:S(2)}) collective-permute-start(f32[2,4,2,16,768]{4,3,2,1,0:T(8,128)} %get-tuple-element.25), channel_id=1, source_target_pairs={{0,4},{1,5},{2,6},{3,7},{4,0},{5,1},{6,2},{7,3},{8,12},{9,13},{10,... | collective-permute-start | bytes 2359304 | tf_op jit(solution)/shard_map/ppermute | solution.py:385
  79.3 10.1 %collective-permute-start.3 = (f32[4,2,16,768]{3,2,1,0:T(8,128)S(1)}, f32[4,2,16,768]{3,2,1,0:T(8,128)S(1)}, u32[]{:S(2)}, u32[]{:S(2)}) collective-permute-start(f32[4,2,16,768]{3,2,1,0:T(8,128)S(1)} %fusion.3), channel_id=1, source_target_pairs={{0,4},{1,5},{2,6},{3,7},{4,0},{5,1},{6,2},{7,3},{8,12},{9,13},{10,... | collective-permute-start | bytes 1179656 | tf_op jit(solution)/shard_map/ppermute | solution.py:385
  82.3 9.7 %collective-permute-start.5 = (f32[4,2,16,768]{3,2,1,0:T(8,128)S(1)}, f32[4,2,16,768]{3,2,1,0:T(8,128)S(1)}, u32[]{:S(2)}, u32[]{:S(2)}) collective-permute-start(f32[4,2,16,768]{3,2,1,0:T(8,128)S(1)} %fusion), channel_id=1, source_target_pairs={{0,1},{1,0},{2,3},{3,2},{4,5},{5,4},{6,7},{7,6},{8,9},{9,8},{10,11... | collective-permute-start | bytes 1179656 | tf_op jit(solution)/shard_map/ppermute | solution.py:385
  93.1 27.3 %all-to-all-start.1 = ((f32[8,16,1536]{2,1,0:T(8,128)}), f32[8,16,1536]{2,1,0:T(8,128)S(1)}, u32[]{:S(2)}, u32[]{:S(2)}) async-start(f32[8,16,1536]{2,1,0:T(8,128)} %bitcast.11), calls=%async_computation.1 | async-start | bytes 1572864 | tf_op jit(solution)/shard_map/all_to_all | solution.py:411
Sparse Core Ops, SparseCore 0:
  57.6 53.8 reduce-scatter.1

commit v6 on v5

--- a/solution.py
+++ b/solution.py
@@ -49,7 +49,7 @@
 
 
 SCORE_STEPS = 3
-SCORE_COPIES = 3 + 4 * SCORE_STEPS
+SCORE_COPIES = 4 + 4 * SCORE_STEPS
 
 
 def score_kernel(
@@ -86,7 +86,9 @@
             first = m + r if k < per else m + n + SPARE + r
             k = k % per
             x_ref[first : first + LANES, k * LANES : (k + 1) * LANES] = block
-    rest = pl.ds(m, x_ref.shape[0] - m)
+    first = pl.ds(m, n + SPARE)
+    out.append(copies.start(x_ref.at[first], x_hbm.at[first]))
+    rest = (pl.ds(m + n + SPARE, n), pl.ds(0, an_ref.shape[1] - n))
     out.append(copies.start(x_ref.at[rest], x_hbm.at[rest]))
     out.append(copies.start(an_ref, an_hbm))
     left = lax.broadcasted_iota(jnp.int32, (rows, LANES), 1) < LANES // 2
@@ -268,7 +270,7 @@
             *(pltpu.VMEM(*s) for s in scratch + outs),
             pltpu.SemaphoreType.DMA((CANDIDATE_COPIES + 2 * CANDIDATE_STEPS,)),
         ],
-        compiler_params=pltpu.CompilerParams(vmem_limit_bytes=60 * MIB),
+        compiler_params=pltpu.CompilerParams(vmem_limit_bytes=32 * MIB),
         name="candidate_terms",
     )(st, other, cot, ag, split(row), split(cc), an, x, y)
 

time: 131 us -> 137 us (1.046)
  local copies, waits for them, and re-layouts: 1.4 us -> 7.46 us
    unnamed x6 -> x16, local copies, waits for them, and re-layouts: 0.6 us -> 6.66 us
where the time goes in v6:
time: 137 us; the launch traced here: 136 us
  waiting for transfers between devices  37.7 us (28%)
  starting transfers between devices  30.9 us (23%)
  Pallas kernels  25 us (18%)
  blocking collectives  16 us (12%)
  between operations  14.2 us (10%)
  local copies, waits for them, and re-layouts  7.46 us (5%)
  other arithmetic  4.23 us (3%)
    all_to_all x1, waiting for transfers between devices, per_device(): lax.all_to_all(terms, 'cand', 0, 0, axis_index_groups=groups, tiled=True)  21.8 us
    ppermute x2, starting transfers between devices, sibling(): return lax.ppermute(v, 'anc', [(p, p ^ 1) for p in range(n_anc)])  16.2 us
    all_to_all x1, blocking collectives, per_device(): st = jnp.sum(lax.all_to_all(st, 'cand', 0, 0, tiled=True), axis=0)  16 us
    ppermute x4, waiting for transfers between devices, swap(): return lax.ppermute(v, ('anc', 'cand'), pairs)  15.3 us
    ppermute x4, starting transfers between devices, swap(): return lax.ppermute(v, ('anc', 'cand'), pairs)  10 us
    pallas_call x1, Pallas kernels, candidate_stage(): pl.pallas_call(candidate_kernel, in_specs=[VMEM] * 4 + [HBM] * 5, out_spe...  8.3 us
    pallas_call x1, Pallas kernels, score_stage(): pl.pallas_call(score_kernel, in_specs=[HBM, HBM, VMEM, VMEM, VMEM], out_s...  7.85 us
    unnamed x16, local copies, waits for them, and re-layouts  6.66 us
  transfers between devices with their start and end apart: 8, of which 5 were waited for; matrix products, arithmetic and copies ran while one was open for 4% of the time, Pallas kernels for 5%

profile of v6, /device:TPU:1, one launch (start us, length us, event | category | flops | bytes accessed | tf_op | source)
XLA Modules:
  0.0 135.5 jit_solution(11454282352485976452)
XLA Ops:
  7.2 7.9 %scores.1 = (bf16[512,768]{1,0:T(8,128)(2,1)}, f32[1992,512]{1,0:T(8,128)}, f32[32,12,128]{2,1,0:T(8,128)}, f32[960,128]{1,0:T(8,128)}, bf16[960,768]{1,0:T(8,128)(2,1)}) custom-call(bf16[512,1536]{1,0:T(8,128)(2,1)} %a_hbm.1, bf16[960,1536]{1,0:T(8,128)(2,1)} %c_hbm.3, s32[1,512]{1,0:T(1,128)} %bitcast.24, s32[1,960]{1,0:T(1,128)} %bitcast.31, ...), custom_call_target="tpu_custom_call" | custom-call | tf_op jit(solution)/shard_map/scores/pallas_call | solution.py:139
  15.1 12.4 %collective-permute-start.1 = (f32[1992,512]{1,0:T(8,128)}, f32[1992,512]{1,0:T(8,128)}, u32[]{:S(2)}, u32[]{:S(2)}) collective-permute-start(f32[1992,512]{1,0:T(8,128)} %get-tuple-element.19.x_hbm), channel_id=1, source_target_pairs={{0,32},{32,0},{64,96},{96,64},{128,160},{160,128},{192,224},{224,1... | collective-permute-start | bytes 12238856 | tf_op jit(solution)/shard_map/ppermute | solution.py:390
  27.5 16.0 %all_to_all.10 = f32[32,12,128]{2,1,0:T(8,128)S(1)} all-to-all(f32[32,12,128]{2,1,0:T(8,128)} %get-tuple-element.15), channel_id=1, replica_groups=mesh['anc'=24,'cand'=32] {'cand'}, dimensions={0} | all-to-all | bytes 393216 | tf_op jit(solution)/shard_map/all_to_all | solution.py:396
  43.6 3.8 %collective-permute-start = (f32[12,128]{1,0:T(8,128)S(1)}, f32[12,128]{1,0:T(8,128)S(1)}, u32[]{:S(2)}, u32[]{:S(2)}) collective-permute-start(f32[12,128]{1,0:T(8,128)S(1)} %reduce_sum.9.st_ref), channel_id=1, source_target_pairs={{0,32},{32,0},{64,96},{96,64},{128,160},{160,128},{192,224},{224,1... | collective-permute-start | bytes 18440 | tf_op jit(solution)/shard_map/ppermute | solution.py:390
  48.0 2.2 %copy-done = f32[1992,512]{1,0:T(8,128)S(1)} copy-done((f32[1992,512]{1,0:T(8,128)S(1)}, f32[1992,512]{1,0:T(8,128)}, u32[]{:S(2)}) %copy-start) | copy-done | bytes 4079640
  50.2 1.4 %copy-done.1 = bf16[960,768]{1,0:T(8,128)(2,1)S(1)} copy-done((bf16[960,768]{1,0:T(8,128)(2,1)S(1)}, bf16[960,768]{1,0:T(8,128)(2,1)}, u32[]{:S(2)}) %copy-start.1) | copy-done | bytes 1474584
  51.5 1.1 copy-done.2
  52.7 1.0 copy-done.3
  53.7 8.3 %candidate_terms.1 = (f32[1,512]{1,0:T(1,128)}, bf16[2,480,512]{2,1,0:T(8,128)(2,1)S(1)}, f32[12,480,128]{2,1,0:T(8,128)}) custom-call(f32[12,128]{1,0:T(8,128)S(1)} %reduce_sum.9.st_ref, f32[12,128]{1,0:T(8,128)S(1)} %collective-permute-done.other_ref, f32[1,512]{1,0:T(1,128)S(1)} %bitcast.27, s32[1,512]{1,0:T(1,128)S(1)} %bitcast.25, ...), custom_call_target="tpu_custom_call" | custom-call | tf_op jit(solution)/shard_map/candidate_terms/pallas_call | solution.py:264
  62.0 1.0 copy-done.6
  63.0 6.1 %anchor_terms.1 = (f32[2,4,2,16,768]{4,3,2,1,0:T(8,128)}, f32[2,4,2,16,768]{4,3,2,1,0:T(8,128)}, f32[2,4,2,16,768]{4,3,2,1,0:T(8,128)}, f32[2,4,2,16,768]{4,3,2,1,0:T(8,128)}) custom-call(bf16[960,512]{1,0:T(8,128)(2,1)} %bitcast.28, f32[960,128]{1,0:T(8,128)} %get-tuple-element.16.row_hbm, bf16[960,1536]{1,0:T(8,128)(2,1)} %c_hbm.3), custom_call_target="tpu_custom_call" | custom-call | flops 1509949440 | bytes 8388608 | tf_op jit(solution)/shard_map/anchor_terms/pallas_call | solution.py:318
  69.1 3.0 %collective-permute-start.2 = (f32[2,4,2,16,768]{4,3,2,1,0:T(8,128)}, f32[2,4,2,16,768]{4,3,2,1,0:T(8,128)S(1)}, u32[]{:S(2)}, u32[]{:S(2)}) collective-permute-start(f32[2,4,2,16,768]{4,3,2,1,0:T(8,128)} %get-tuple-element.23), channel_id=1, source_target_pairs={{0,1},{1,0},{2,3},{3,2},{4,5},{5,4},{6,7},{7,6},{8,9},{9,8},{10,11... | collective-permute-start | bytes 2359304 | tf_op jit(solution)/shard_map/ppermute | solution.py:387
  72.2 1.9 %collective-permute-start.4 = (f32[2,4,2,16,768]{4,3,2,1,0:T(8,128)}, f32[2,4,2,16,768]{4,3,2,1,0:T(8,128)S(1)}, u32[]{:S(2)}, u32[]{:S(2)}) collective-permute-start(f32[2,4,2,16,768]{4,3,2,1,0:T(8,128)} %get-tuple-element.25), channel_id=1, source_target_pairs={{0,4},{1,5},{2,6},{3,7},{4,0},{5,1},{6,2},{7,3},{8,12},{9,13},{10,... | collective-permute-start | bytes 2359304 | tf_op jit(solution)/shard_map/ppermute | solution.py:387
  74.1 9.7 %collective-permute-done.2 = f32[2,4,2,16,768]{4,3,2,1,0:T(8,128)S(1)} collective-permute-done((f32[2,4,2,16,768]{4,3,2,1,0:T(8,128)}, f32[2,4,2,16,768]{4,3,2,1,0:T(8,128)S(1)}, u32[]{:S(2)}, u32[]{:S(2)}) %collective-permute-start.2) | collective-permute-done | bytes 786464 | tf_op jit(solution)/shard_map/ppermute | solution.py:387
  83.8 1.0 fusion.3
  84.9 1.9 %collective-permute-start.3 = (f32[4,2,16,768]{3,2,1,0:T(8,128)S(1)}, f32[4,2,16,768]{3,2,1,0:T(8,128)S(1)}, u32[]{:S(2)}, u32[]{:S(2)}) collective-permute-start(f32[4,2,16,768]{3,2,1,0:T(8,128)S(1)} %fusion.3), channel_id=1, source_target_pairs={{0,4},{1,5},{2,6},{3,7},{4,0},{5,1},{6,2},{7,3},{8,12},{9,13},{10,... | collective-permute-start | bytes 1179656 | tf_op jit(solution)/shard_map/ppermute | solution.py:387
  86.8 1.1 fusion
  87.9 3.1 %collective-permute-start.5 = (f32[4,2,16,768]{3,2,1,0:T(8,128)S(1)}, f32[4,2,16,768]{3,2,1,0:T(8,128)S(1)}, u32[]{:S(2)}, u32[]{:S(2)}) collective-permute-start(f32[4,2,16,768]{3,2,1,0:T(8,128)S(1)} %fusion), channel_id=1, source_target_pairs={{0,1},{1,0},{2,3},{3,2},{4,5},{5,4},{6,7},{7,6},{8,9},{9,8},{10,11... | collective-permute-start | bytes 1179656 | tf_op jit(solution)/shard_map/ppermute | solution.py:387
  91.0 4.0 %collective-permute-done.3 = f32[4,2,16,768]{3,2,1,0:T(8,128)S(1)} collective-permute-done((f32[4,2,16,768]{3,2,1,0:T(8,128)S(1)}, f32[4,2,16,768]{3,2,1,0:T(8,128)S(1)}, u32[]{:S(2)}, u32[]{:S(2)}) %collective-permute-start.3) | collective-permute-done | bytes 393248 | tf_op jit(solution)/shard_map/ppermute | solution.py:387
  95.0 1.1 fusion.5
  96.1 1.5 %collective-permute-done.5 = f32[4,2,16,768]{3,2,1,0:T(8,128)S(1)} collective-permute-done((f32[4,2,16,768]{3,2,1,0:T(8,128)S(1)}, f32[4,2,16,768]{3,2,1,0:T(8,128)S(1)}, u32[]{:S(2)}, u32[]{:S(2)}) %collective-permute-start.5) | collective-permute-done | bytes 393248 | tf_op jit(solution)/shard_map/ppermute | solution.py:387
  98.6 4.7 %all-to-all-start.1 = ((f32[8,16,1536]{2,1,0:T(8,128)}), f32[8,16,1536]{2,1,0:T(8,128)S(1)}, u32[]{:S(2)}, u32[]{:S(2)}) async-start(f32[8,16,1536]{2,1,0:T(8,128)} %bitcast.11), calls=%async_computation.1 | async-start | bytes 1572864 | tf_op jit(solution)/shard_map/all_to_all | solution.py:413
  104.1 21.8 %all-to-all-done.1.t_ref = f32[8,16,1536]{2,1,0:T(8,128)S(1)} async-done(((f32[8,16,1536]{2,1,0:T(8,128)}), f32[8,16,1536]{2,1,0:T(8,128)S(1)}, u32[]{:S(2)}, u32[]{:S(2)}) %all-to-all-start.1) | async-done | bytes 786464 | tf_op jit(solution)/shard_map/all_to_all | solution.py:413
  126.8 1.9 %unpack.1 = f32[64,960]{1,0:T(8,128)} custom-call(f32[480,128]{1,0:T(8,128)} %bitcast.30), custom_call_target="tpu_custom_call" | custom-call | tf_op jit(solution)/shard_map/unpack/pallas_call | solution.py:364
  (22 shorter events, 3.4 us)
Async XLA Ops:
  7.2 40.8 %copy-start.4 = (s32[512]{0:T(512)S(1)}, s32[512]{0:T(512)}, u32[]{:S(2)}) copy-start(s32[512]{0:T(512)} %param.7) | copy-start | bytes 6148
  7.2 40.8 %copy-start.5 = (f32[512]{0:T(512)S(1)}, f32[512]{0:T(512)}, u32[]{:S(2)}) copy-start(f32[512]{0:T(512)} %param.9) | copy-start | bytes 6148
  7.2 119.6 %reduce-scatter.2.cloned.1.call-start = ((), (), s32[]{:S(2)}) async-start(), calls=%async_computation.3 | async-start | bytes 3194880 | tf_op jit(solution)/shard_map/reduce_scatter | solution.py:398
  15.1 32.9 %collective-permute-start.1 = (f32[1992,512]{1,0:T(8,128)}, f32[1992,512]{1,0:T(8,128)}, u32[]{:S(2)}, u32[]{:S(2)}) collective-permute-start(f32[1992,512]{1,0:T(8,128)} %get-tuple-element.19.x_hbm), channel_id=1, source_target_pairs={{0,32},{32,0},{64,96},{96,64},{128,160},{160,128},{192,224},{224,1... | collective-permute-start | bytes 12238856 | tf_op jit(solution)/shard_map/ppermute | solution.py:390
  43.6 4.4 %collective-permute-start = (f32[12,128]{1,0:T(8,128)S(1)}, f32[12,128]{1,0:T(8,128)S(1)}, u32[]{:S(2)}, u32[]{:S(2)}) collective-permute-start(f32[12,128]{1,0:T(8,128)S(1)} %reduce_sum.9.st_ref), channel_id=1, source_target_pairs={{0,32},{32,0},{64,96},{96,64},{128,160},{160,128},{192,224},{224,1... | collective-permute-start | bytes 18440 | tf_op jit(solution)/shard_map/ppermute | solution.py:390
  48.0 2.2 %copy-start = (f32[1992,512]{1,0:T(8,128)S(1)}, f32[1992,512]{1,0:T(8,128)}, u32[]{:S(2)}) copy-start(f32[1992,512]{1,0:T(8,128)} %get-tuple-element.19.x_hbm) | copy-start | bytes 12238852
  50.2 1.4 %copy-start.1 = (bf16[960,768]{1,0:T(8,128)(2,1)S(1)}, bf16[960,768]{1,0:T(8,128)(2,1)}, u32[]{:S(2)}) copy-start(bf16[960,768]{1,0:T(8,128)(2,1)} %get-tuple-element.17) | copy-start | bytes 4423684
  51.5 1.1 copy-start.2
  52.7 1.0 copy-start.3
  62.0 1.0 copy-start.6
  69.1 28.5 %copy-start.7 = (f32[2,4,2,16,768]{4,3,2,1,0:T(8,128)S(1)}, f32[2,4,2,16,768]{4,3,2,1,0:T(8,128)}, u32[]{:S(2)}) copy-start(f32[2,4,2,16,768]{4,3,2,1,0:T(8,128)} %get-tuple-element.24) | copy-start | bytes 2359300
  69.1 14.7 %collective-permute-start.2 = (f32[2,4,2,16,768]{4,3,2,1,0:T(8,128)}, f32[2,4,2,16,768]{4,3,2,1,0:T(8,128)S(1)}, u32[]{:S(2)}, u32[]{:S(2)}) collective-permute-start(f32[2,4,2,16,768]{4,3,2,1,0:T(8,128)} %get-tuple-element.23), channel_id=1, source_target_pairs={{0,1},{1,0},{2,3},{3,2},{4,5},{5,4},{6,7},{7,6},{8,9},{9,8},{10,11... | collective-permute-start | bytes 2359304 | tf_op jit(solution)/shard_map/ppermute | solution.py:387
  72.2 14.6 %collective-permute-start.4 = (f32[2,4,2,16,768]{4,3,2,1,0:T(8,128)}, f32[2,4,2,16,768]{4,3,2,1,0:T(8,128)S(1)}, u32[]{:S(2)}, u32[]{:S(2)}) collective-permute-start(f32[2,4,2,16,768]{4,3,2,1,0:T(8,128)} %get-tuple-element.25), channel_id=1, source_target_pairs={{0,4},{1,5},{2,6},{3,7},{4,0},{5,1},{6,2},{7,3},{8,12},{9,13},{10,... | collective-permute-start | bytes 2359304 | tf_op jit(solution)/shard_map/ppermute | solution.py:387
  84.9 10.1 %collective-permute-start.3 = (f32[4,2,16,768]{3,2,1,0:T(8,128)S(1)}, f32[4,2,16,768]{3,2,1,0:T(8,128)S(1)}, u32[]{:S(2)}, u32[]{:S(2)}) collective-permute-start(f32[4,2,16,768]{3,2,1,0:T(8,128)S(1)} %fusion.3), channel_id=1, source_target_pairs={{0,4},{1,5},{2,6},{3,7},{4,0},{5,1},{6,2},{7,3},{8,12},{9,13},{10,... | collective-permute-start | bytes 1179656 | tf_op jit(solution)/shard_map/ppermute | solution.py:387
  87.9 9.7 %collective-permute-start.5 = (f32[4,2,16,768]{3,2,1,0:T(8,128)S(1)}, f32[4,2,16,768]{3,2,1,0:T(8,128)S(1)}, u32[]{:S(2)}, u32[]{:S(2)}) collective-permute-start(f32[4,2,16,768]{3,2,1,0:T(8,128)S(1)} %fusion), channel_id=1, source_target_pairs={{0,1},{1,0},{2,3},{3,2},{4,5},{5,4},{6,7},{7,6},{8,9},{9,8},{10,11... | collective-permute-start | bytes 1179656 | tf_op jit(solution)/shard_map/ppermute | solution.py:387
  98.6 27.3 %all-to-all-start.1 = ((f32[8,16,1536]{2,1,0:T(8,128)}), f32[8,16,1536]{2,1,0:T(8,128)S(1)}, u32[]{:S(2)}, u32[]{:S(2)}) async-start(f32[8,16,1536]{2,1,0:T(8,128)} %bitcast.11), calls=%async_computation.1 | async-start | bytes 1572864 | tf_op jit(solution)/shard_map/all_to_all | solution.py:413
Sparse Core Ops, SparseCore 0:
  63.1 53.9 reduce-scatter.1

commit v7 on v6

--- a/solution.py
+++ b/solution.py
@@ -270,7 +270,7 @@
             *(pltpu.VMEM(*s) for s in scratch + outs),
             pltpu.SemaphoreType.DMA((CANDIDATE_COPIES + 2 * CANDIDATE_STEPS,)),
         ],
-        compiler_params=pltpu.CompilerParams(vmem_limit_bytes=32 * MIB),
+        compiler_params=pltpu.CompilerParams(vmem_limit_bytes=62 * MIB),
         name="candidate_terms",
     )(st, other, cot, ag, split(row), split(cc), an, x, y)
 

time: 137 us -> 131 us (0.956)
  local copies, waits for them, and re-layouts: 7.46 us -> 1.4 us
    unnamed x16 -> x6, local copies, waits for them, and re-layouts: 6.66 us -> 0.6 us
where the time goes in v7:
time: 131 us
  waiting for transfers between devices  38.5 us (29%)
  starting transfers between devices  31 us (24%)
  Pallas kernels  25.4 us (19%)
  blocking collectives  16 us (12%)
  between operations  14.1 us (11%)
  other arithmetic  4.25 us (3%)
  local copies, waits for them, and re-layouts  1.4 us (1%)
    all_to_all x1, waiting for transfers between devices, per_device(): lax.all_to_all(terms, 'cand', 0, 0, axis_index_groups=groups, tiled=True)  22.6 us
    ppermute x2, starting transfers between devices, sibling(): return lax.ppermute(v, 'anc', [(p, p ^ 1) for p in range(n_anc)])  16.3 us
    all_to_all x1, blocking collectives, per_device(): st = jnp.sum(lax.all_to_all(st, 'cand', 0, 0, tiled=True), axis=0)  16 us
    ppermute x4, waiting for transfers between devices, swap(): return lax.ppermute(v, ('anc', 'cand'), pairs)  15.3 us
    ppermute x4, starting transfers between devices, swap(): return lax.ppermute(v, ('anc', 'cand'), pairs)  9.99 us
    pallas_call x1, Pallas kernels, candidate_stage(): pl.pallas_call(candidate_kernel, in_specs=[VMEM] * 4 + [HBM] * 5, out_spe...  8.83 us
    pallas_call x1, Pallas kernels, score_stage(): pl.pallas_call(score_kernel, in_specs=[HBM, HBM, VMEM, VMEM, VMEM], out_s...  7.8 us
    pallas_call x1, Pallas kernels, anchor_stage(): pl.pallas_call(anchor_kernel, in_specs=[HBM, HBM, HBM], out_specs=[HBM] *...  6.08 us
  transfers between devices with their start and end apart: 8, of which 5 were waited for; matrix products, arithmetic and copies ran while one was open for 4% of the time, Pallas kernels for 5%

profile of v7, /device:TPU:1, one launch (start us, length us, event | category | flops | bytes accessed | tf_op | source)
XLA Modules:
  0.0 130.8 jit_solution(3656290233805563067)
XLA Ops:
  7.2 7.8 %scores.1 = (bf16[512,768]{1,0:T(8,128)(2,1)}, f32[1992,512]{1,0:T(8,128)}, f32[32,12,128]{2,1,0:T(8,128)}, f32[960,128]{1,0:T(8,128)}, bf16[960,768]{1,0:T(8,128)(2,1)}) custom-call(bf16[512,1536]{1,0:T(8,128)(2,1)} %a_hbm.1, bf16[960,1536]{1,0:T(8,128)(2,1)} %c_hbm.3, s32[1,512]{1,0:T(1,128)} %bitcast.26, s32[1,960]{1,0:T(1,128)} %bitcast.30, ...), custom_call_target="tpu_custom_call" | custom-call | tf_op jit(solution)/shard_map/scores/pallas_call | solution.py:139
  15.0 12.5 %collective-permute-start.1 = (f32[1992,512]{1,0:T(8,128)}, f32[1992,512]{1,0:T(8,128)}, u32[]{:S(2)}, u32[]{:S(2)}) collective-permute-start(f32[1992,512]{1,0:T(8,128)} %get-tuple-element.19.x_hbm), channel_id=1, source_target_pairs={{0,32},{32,0},{64,96},{96,64},{128,160},{160,128},{192,224},{224,1... | collective-permute-start | bytes 12238856 | tf_op jit(solution)/shard_map/ppermute | solution.py:390
  27.5 16.0 %all_to_all.10 = f32[32,12,128]{2,1,0:T(8,128)S(1)} all-to-all(f32[32,12,128]{2,1,0:T(8,128)} %get-tuple-element.15), channel_id=1, replica_groups=mesh['anc'=24,'cand'=32] {'cand'}, dimensions={0} | all-to-all | bytes 393216 | tf_op jit(solution)/shard_map/all_to_all | solution.py:396
  43.6 3.8 %collective-permute-start = (f32[12,128]{1,0:T(8,128)S(1)}, f32[12,128]{1,0:T(8,128)S(1)}, u32[]{:S(2)}, u32[]{:S(2)}) collective-permute-start(f32[12,128]{1,0:T(8,128)S(1)} %reduce_sum.9.st_ref), channel_id=1, source_target_pairs={{0,32},{32,0},{64,96},{96,64},{128,160},{160,128},{192,224},{224,1... | collective-permute-start | bytes 18440 | tf_op jit(solution)/shard_map/ppermute | solution.py:390
  47.4 0.6 collective-permute-done.other_ref
  48.0 0.6 copy-done.2
  48.6 8.8 %candidate_terms.1 = (f32[1,512]{1,0:T(1,128)}, bf16[2,480,512]{2,1,0:T(8,128)(2,1)}, f32[12,480,128]{2,1,0:T(8,128)}) custom-call(f32[12,128]{1,0:T(8,128)} %copy-done.1, f32[12,128]{1,0:T(8,128)} %copy-done.2, f32[1,512]{1,0:T(1,128)} %bitcast.29, s32[1,512]{1,0:T(1,128)} %bitcast.27, f32[2,480,128]{2,1,0:T(8,128)} %bitcast.23, ...), custom_call_target="tpu_custom_call" | custom-call | tf_op jit(solution)/shard_map/candidate_terms/pallas_call | solution.py:264
  57.5 6.1 %anchor_terms.1 = (f32[2,4,2,16,768]{4,3,2,1,0:T(8,128)}, f32[2,4,2,16,768]{4,3,2,1,0:T(8,128)}, f32[2,4,2,16,768]{4,3,2,1,0:T(8,128)}, f32[2,4,2,16,768]{4,3,2,1,0:T(8,128)}) custom-call(bf16[960,512]{1,0:T(8,128)(2,1)} %bitcast.31, f32[960,128]{1,0:T(8,128)} %get-tuple-element.16.row_hbm, bf16[960,1536]{1,0:T(8,128)(2,1)} %c_hbm.3), custom_call_target="tpu_custom_call" | custom-call | flops 1509949440 | bytes 8388608 | tf_op jit(solution)/shard_map/anchor_terms/pallas_call | solution.py:318
  63.6 3.0 %collective-permute-start.2 = (f32[2,4,2,16,768]{4,3,2,1,0:T(8,128)}, f32[2,4,2,16,768]{4,3,2,1,0:T(8,128)S(1)}, u32[]{:S(2)}, u32[]{:S(2)}) collective-permute-start(f32[2,4,2,16,768]{4,3,2,1,0:T(8,128)} %get-tuple-element.23), channel_id=1, source_target_pairs={{0,1},{1,0},{2,3},{3,2},{4,5},{5,4},{6,7},{7,6},{8,9},{9,8},{10,11... | collective-permute-start | bytes 2359304 | tf_op jit(solution)/shard_map/ppermute | solution.py:387
  66.6 1.9 %collective-permute-start.4 = (f32[2,4,2,16,768]{4,3,2,1,0:T(8,128)}, f32[2,4,2,16,768]{4,3,2,1,0:T(8,128)S(1)}, u32[]{:S(2)}, u32[]{:S(2)}) collective-permute-start(f32[2,4,2,16,768]{4,3,2,1,0:T(8,128)} %get-tuple-element.25), channel_id=1, source_target_pairs={{0,4},{1,5},{2,6},{3,7},{4,0},{5,1},{6,2},{7,3},{8,12},{9,13},{10,... | collective-permute-start | bytes 2359304 | tf_op jit(solution)/shard_map/ppermute | solution.py:387
  68.6 9.7 %collective-permute-done.2 = f32[2,4,2,16,768]{4,3,2,1,0:T(8,128)S(1)} collective-permute-done((f32[2,4,2,16,768]{4,3,2,1,0:T(8,128)}, f32[2,4,2,16,768]{4,3,2,1,0:T(8,128)S(1)}, u32[]{:S(2)}, u32[]{:S(2)}) %collective-permute-start.2) | collective-permute-done | bytes 786464 | tf_op jit(solution)/shard_map/ppermute | solution.py:387
  78.3 1.0 fusion.3
  79.3 1.9 %collective-permute-start.3 = (f32[4,2,16,768]{3,2,1,0:T(8,128)S(1)}, f32[4,2,16,768]{3,2,1,0:T(8,128)S(1)}, u32[]{:S(2)}, u32[]{:S(2)}) collective-permute-start(f32[4,2,16,768]{3,2,1,0:T(8,128)S(1)} %fusion.3), channel_id=1, source_target_pairs={{0,4},{1,5},{2,6},{3,7},{4,0},{5,1},{6,2},{7,3},{8,12},{9,13},{10,... | collective-permute-start | bytes 1179656 | tf_op jit(solution)/shard_map/ppermute | solution.py:387
  81.3 1.1 fusion
  82.3 3.1 %collective-permute-start.5 = (f32[4,2,16,768]{3,2,1,0:T(8,128)S(1)}, f32[4,2,16,768]{3,2,1,0:T(8,128)S(1)}, u32[]{:S(2)}, u32[]{:S(2)}) collective-permute-start(f32[4,2,16,768]{3,2,1,0:T(8,128)S(1)} %fusion), channel_id=1, source_target_pairs={{0,1},{1,0},{2,3},{3,2},{4,5},{5,4},{6,7},{7,6},{8,9},{9,8},{10,11... | collective-permute-start | bytes 1179656 | tf_op jit(solution)/shard_map/ppermute | solution.py:387
  85.5 4.0 %collective-permute-done.3 = f32[4,2,16,768]{3,2,1,0:T(8,128)S(1)} collective-permute-done((f32[4,2,16,768]{3,2,1,0:T(8,128)S(1)}, f32[4,2,16,768]{3,2,1,0:T(8,128)S(1)}, u32[]{:S(2)}, u32[]{:S(2)}) %collective-permute-start.3) | collective-permute-done | bytes 393248 | tf_op jit(solution)/shard_map/ppermute | solution.py:387
  89.5 1.1 fusion.5
  90.5 1.5 %collective-permute-done.5 = f32[4,2,16,768]{3,2,1,0:T(8,128)S(1)} collective-permute-done((f32[4,2,16,768]{3,2,1,0:T(8,128)S(1)}, f32[4,2,16,768]{3,2,1,0:T(8,128)S(1)}, u32[]{:S(2)}, u32[]{:S(2)}) %collective-permute-start.5) | collective-permute-done | bytes 393248 | tf_op jit(solution)/shard_map/ppermute | solution.py:387
  92.1 1.0 pad_maximum_fusion
  93.1 4.7 %all-to-all-start.1 = ((f32[8,16,1536]{2,1,0:T(8,128)}), f32[8,16,1536]{2,1,0:T(8,128)S(1)}, u32[]{:S(2)}, u32[]{:S(2)}) async-start(f32[8,16,1536]{2,1,0:T(8,128)} %bitcast.11), calls=%async_computation.1 | async-start | bytes 1572864 | tf_op jit(solution)/shard_map/all_to_all | solution.py:413
  97.8 0.8 constant_dynamic-slice_fusion.a_ref
  98.6 22.6 %all-to-all-done.1.t_ref = f32[8,16,1536]{2,1,0:T(8,128)S(1)} async-done(((f32[8,16,1536]{2,1,0:T(8,128)}), f32[8,16,1536]{2,1,0:T(8,128)S(1)}, u32[]{:S(2)}, u32[]{:S(2)}) %all-to-all-start.1) | async-done | bytes 786464 | tf_op jit(solution)/shard_map/all_to_all | solution.py:413
  121.2 0.8 probe_derivatives.1
  122.1 1.9 %unpack.1 = f32[64,960]{1,0:T(8,128)} custom-call(f32[480,128]{1,0:T(8,128)} %bitcast.25), custom_call_target="tpu_custom_call" | custom-call | tf_op jit(solution)/shard_map/unpack/pallas_call | solution.py:364
  (12 shorter events, 0.2 us)
Async XLA Ops:
  7.2 114.9 %reduce-scatter.2.cloned.1.call-start = ((), (), s32[]{:S(2)}) async-start(), calls=%async_computation.3 | async-start | bytes 3194880 | tf_op jit(solution)/shard_map/reduce_scatter | solution.py:398
  15.0 33.0 %collective-permute-start.1 = (f32[1992,512]{1,0:T(8,128)}, f32[1992,512]{1,0:T(8,128)}, u32[]{:S(2)}, u32[]{:S(2)}) collective-permute-start(f32[1992,512]{1,0:T(8,128)} %get-tuple-element.19.x_hbm), channel_id=1, source_target_pairs={{0,32},{32,0},{64,96},{96,64},{128,160},{160,128},{192,224},{224,1... | collective-permute-start | bytes 12238856 | tf_op jit(solution)/shard_map/ppermute | solution.py:390
  43.6 4.5 %copy-start.1 = (f32[12,128]{1,0:T(8,128)}, f32[12,128]{1,0:T(8,128)S(1)}, u32[]{:S(2)}) copy-start(f32[12,128]{1,0:T(8,128)S(1)} %reduce_sum.9.st_ref) | copy-start | bytes 18436
  43.6 4.4 %collective-permute-start = (f32[12,128]{1,0:T(8,128)S(1)}, f32[12,128]{1,0:T(8,128)S(1)}, u32[]{:S(2)}, u32[]{:S(2)}) collective-permute-start(f32[12,128]{1,0:T(8,128)S(1)} %reduce_sum.9.st_ref), channel_id=1, source_target_pairs={{0,32},{32,0},{64,96},{96,64},{128,160},{160,128},{192,224},{224,1... | collective-permute-start | bytes 18440 | tf_op jit(solution)/shard_map/ppermute | solution.py:390
  48.0 0.6 copy-start.2
  63.6 28.5 %copy-start = (f32[2,4,2,16,768]{4,3,2,1,0:T(8,128)S(1)}, f32[2,4,2,16,768]{4,3,2,1,0:T(8,128)}, u32[]{:S(2)}) copy-start(f32[2,4,2,16,768]{4,3,2,1,0:T(8,128)} %get-tuple-element.24) | copy-start | bytes 2359300
  63.6 14.7 %collective-permute-start.2 = (f32[2,4,2,16,768]{4,3,2,1,0:T(8,128)}, f32[2,4,2,16,768]{4,3,2,1,0:T(8,128)S(1)}, u32[]{:S(2)}, u32[]{:S(2)}) collective-permute-start(f32[2,4,2,16,768]{4,3,2,1,0:T(8,128)} %get-tuple-element.23), channel_id=1, source_target_pairs={{0,1},{1,0},{2,3},{3,2},{4,5},{5,4},{6,7},{7,6},{8,9},{9,8},{10,11... | collective-permute-start | bytes 2359304 | tf_op jit(solution)/shard_map/ppermute | solution.py:387
  66.6 14.6 %collective-permute-start.4 = (f32[2,4,2,16,768]{4,3,2,1,0:T(8,128)}, f32[2,4,2,16,768]{4,3,2,1,0:T(8,128)S(1)}, u32[]{:S(2)}, u32[]{:S(2)}) collective-permute-start(f32[2,4,2,16,768]{4,3,2,1,0:T(8,128)} %get-tuple-element.25), channel_id=1, source_target_pairs={{0,4},{1,5},{2,6},{3,7},{4,0},{5,1},{6,2},{7,3},{8,12},{9,13},{10,... | collective-permute-start | bytes 2359304 | tf_op jit(solution)/shard_map/ppermute | solution.py:387
  79.3 10.1 %collective-permute-start.3 = (f32[4,2,16,768]{3,2,1,0:T(8,128)S(1)}, f32[4,2,16,768]{3,2,1,0:T(8,128)S(1)}, u32[]{:S(2)}, u32[]{:S(2)}) collective-permute-start(f32[4,2,16,768]{3,2,1,0:T(8,128)S(1)} %fusion.3), channel_id=1, source_target_pairs={{0,4},{1,5},{2,6},{3,7},{4,0},{5,1},{6,2},{7,3},{8,12},{9,13},{10,... | collective-permute-start | bytes 1179656 | tf_op jit(solution)/shard_map/ppermute | solution.py:387
  82.3 9.7 %collective-permute-start.5 = (f32[4,2,16,768]{3,2,1,0:T(8,128)S(1)}, f32[4,2,16,768]{3,2,1,0:T(8,128)S(1)}, u32[]{:S(2)}, u32[]{:S(2)}) collective-permute-start(f32[4,2,16,768]{3,2,1,0:T(8,128)S(1)} %fusion), channel_id=1, source_target_pairs={{0,1},{1,0},{2,3},{3,2},{4,5},{5,4},{6,7},{7,6},{8,9},{9,8},{10,11... | collective-permute-start | bytes 1179656 | tf_op jit(solution)/shard_map/ppermute | solution.py:387
  93.1 28.1 %all-to-all-start.1 = ((f32[8,16,1536]{2,1,0:T(8,128)}), f32[8,16,1536]{2,1,0:T(8,128)S(1)}, u32[]{:S(2)}, u32[]{:S(2)}) async-start(f32[8,16,1536]{2,1,0:T(8,128)} %bitcast.11), calls=%async_computation.1 | async-start | bytes 1572864 | tf_op jit(solution)/shard_map/all_to_all | solution.py:413
Sparse Core Ops, SparseCore 0:
  57.6 53.9 reduce-scatter.1
